TPU v7x, 32 devices: a whole 2x2x4 slice. The times are simulated.
32 devices in a mesh: dp: 16 (over z, y, x), mp: 2 (over core).
Axes of the slice: x: 2, y: 2, z: 4, core: 2. Of those that a mesh axis runs over, the one named last changes fastest.
Arguments:
- hidden_in: bfloat16 [4096, 1472], P(('dp', 'mp')), may hold values from -6 to 6
- attention_gain: float32 [1472], replicated, may hold values from 0.25 to 1.75
- query_weight: bfloat16 [1472, 384], P(None, 'mp'), may hold values from -0.078125 to 0.078125
- key_weight: bfloat16 [1472, 384], P(None, 'mp'), may hold values from -0.078125 to 0.078125
- value_weight: bfloat16 [1472, 384], P(None, 'mp'), may hold values from -0.15625 to 0.15625
- output_weight: bfloat16 [384, 1472], P('mp'), may hold values from -0.875 to 0.875
- position_bias: float32 [32, 6], P(None, 'mp'), may hold values from -4 to 4
- feedforward_gain: float32 [1472], replicated, may hold values from 0.25 to 1.75
- gate_weight: bfloat16 [1472, 3584], P(None, 'mp'), may hold values from -0.15625 to 0.15625
- up_weight: bfloat16 [1472, 3584], P(None, 'mp'), may hold values from -0.15625 to 0.15625
- down_weight: bfloat16 [3584, 1472], P('mp'), may hold values from -0.125 to 0.125
- cotangent: bfloat16 [4096, 1472], P(('dp', 'mp')), may hold values from -6 to 6
- item_lengths: int32 [16], replicated, may hold values from 1 to 256, 2560 in all
- item_group: int32 [16], replicated, may hold values from 0 to 15, each once
- bucket_ids: int32 [511], replicated, may hold values from 0 to 31, as said below
Outputs:
- layer_out: float32 [4096, 1472], P(('dp', 'mp'))
- input_grad: float32 [4096, 1472], P(('dp', 'mp'))
- attention_gain_grad: float32 [1472], replicated
- query_grad: float32 [1472, 384], P('dp', 'mp')
- key_grad: float32 [1472, 384], P('dp', 'mp')
- value_grad: float32 [1472, 384], P('dp', 'mp')
- output_grad: float32 [384, 1472], P('mp', 'dp')
- position_bias_grad: float32 [32, 6], P(None, 'mp')
- feedforward_gain_grad: float32 [1472], replicated
- gate_grad: float32 [1472, 3584], P('dp', 'mp')
- up_grad: float32 [1472, 3584], P('dp', 'mp')
- down_grad: float32 [3584, 1472], P('mp', 'dp')
Inputs may be any that keep to these rules, and one draw needn't show every extreme that they name: `item_lengths`: the lengths sum to 2560, and one of them is exactly 256. `item_group`: each group number appears once. `bucket_ids`: entry r + 255 is the bucket of a key r positions after its query: 0 at r = 0, never falling as |r| grows for one sign of r, 16 or more exactly where r > 0, and 31 at r = 255.
All inputs are finite; a program needn't handle non-finite values.
Results may differ from a plain program's by a relative error of at most 0.025.
Values may be sent and summed in bfloat16 or wider, within the bound.
A program may use at most 192 MiB of HBM per device.

v0:
```python
import jax
import jax.numpy as jnp
from jax import lax
from jax.sharding import PartitionSpec as P

DKV = 64


norm_epsilon = 1e-06


def norm_parts(row_vals, gain_vec):
    inv_rms = lax.rsqrt(jnp.mean(row_vals * row_vals, axis=1, keepdims=True) + norm_epsilon)
    unit_rows = row_vals * inv_rms
    return (inv_rms, unit_rows, (unit_rows * gain_vec).astype(jnp.bfloat16))


def norm_back(grad_normed, inv_rms, unit_rows, gain_vec):
    grad_unit = grad_normed * gain_vec
    inner = jnp.mean(grad_unit * unit_rows, axis=1, keepdims=True)
    return (inv_rms * (grad_unit - unit_rows * inner), jnp.sum(grad_normed * unit_rows, axis=0))


def contract_rows(left, right):
    return lax.dot_general(
        left, right, (((0,), (0,)), ((), ())), preferred_element_type=jnp.float32
    )


def contract_cols(left, right):
    return lax.dot_general(
        left, right, (((1,), (1,)), ((), ())), preferred_element_type=jnp.float32
    )


def add_diagonals(diag_sums, grad_scores, first_row):
    head_count = grad_scores.shape[0]
    block_rows = grad_scores.shape[1]
    seq_len = grad_scores.shape[2]
    padded_width = block_rows + seq_len
    padded = jnp.concatenate(
        [jnp.zeros((head_count, block_rows, block_rows), jnp.float32), grad_scores], axis=2
    )
    flattened = padded.reshape(head_count, block_rows * padded_width)
    flattened = jnp.concatenate(
        [flattened, jnp.zeros((head_count, block_rows), jnp.float32)], axis=1
    )
    skewed = flattened.reshape(head_count, block_rows, padded_width + 1)
    column_sums = jnp.sum(skewed, axis=1)
    begin = seq_len - 1 - first_row
    current = lax.dynamic_slice_in_dim(diag_sums, begin, padded_width + 1, 1)
    return lax.dynamic_update_slice_in_dim(diag_sums, current + column_sums, begin, 1)


def shards(
    hidden_in,
    attention_gain,
    query_weight,
    key_weight,
    value_weight,
    output_weight,
    position_bias,
    feedforward_gain,
    gate_weight,
    up_weight,
    down_weight,
    cotangent,
    item_lengths,
    item_group,
    bucket_ids,
):
    local_rows = hidden_in.shape[0]
    seq_len = local_rows * lax.axis_size("mp")
    head_width = query_weight.shape[1]
    local_heads = head_width // DKV
    block_rows = min(512, seq_len)
    block_count = seq_len // block_rows
    group_len = jnp.sum(jnp.where(item_group == lax.axis_index("dp"), item_lengths, 0))
    positions = jnp.arange(seq_len, dtype=jnp.int32)
    key_valid = positions < group_len
    row_valid = (
        lax.axis_index("mp") * local_rows + jnp.arange(local_rows, dtype=jnp.int32) < group_len
    )
    residual = hidden_in.astype(jnp.float32)
    inv_one, unit_one, normed_one = norm_parts(residual, attention_gain)
    gathered_one = lax.all_gather(normed_one, "mp", axis=0, tiled=True)
    joined_weight = jnp.concatenate([query_weight, key_weight, value_weight], axis=1)
    projected = jnp.dot(gathered_one, joined_weight, preferred_element_type=jnp.float32).astype(
        jnp.bfloat16
    )
    queries = projected[:, :head_width].reshape(seq_len, local_heads, DKV)
    key_rows = projected[:, head_width : 2 * head_width].reshape(seq_len, local_heads, DKV)
    values = projected[:, 2 * head_width :].reshape(seq_len, local_heads, DKV)
    onehot = (
        bucket_ids[:, None] == jnp.arange(position_bias.shape[0], dtype=jnp.int32)[None, :]
    ).astype(jnp.float32)
    bias_by_offset = jnp.dot(onehot, position_bias, precision=lax.Precision.HIGHEST).T

    def block_scores(first_row):
        raw_scores = jnp.einsum(
            "qhd,khd->hqk", queries, key_rows, preferred_element_type=jnp.float32
        )
        offsets = (
            positions[None, :]
            - (first_row + jnp.arange(block_rows, dtype=jnp.int32))[:, None]
            + seq_len
            - 1
        )
        bias_rows = jnp.take(bias_by_offset, offsets, axis=1)
        return (queries, jnp.where(key_valid[None, None, :], raw_scores + bias_rows, -1e30))

    def forward_block(first_row):
        scores = block_scores(first_row)[1]
        row_peak = jnp.max(scores, axis=2, keepdims=True)
        row_total = jnp.sum(jnp.exp(scores - row_peak), axis=2, keepdims=True)
        log_total = row_peak + jnp.log(row_total)
        probabilities = jnp.exp(scores - log_total).astype(jnp.bfloat16)
        mixed_rows = jnp.einsum(
            "hqk,khd->qhd", probabilities, values, preferred_element_type=jnp.float32
        )
        return (mixed_rows.astype(jnp.bfloat16), log_total[:, :, 0])

    block_starts = jnp.arange(block_count, dtype=jnp.int32) * block_rows
    mixed_blocks, log_totals = lax.map(forward_block, block_starts)
    attended = mixed_blocks.reshape(seq_len, head_width)
    middle = residual + lax.psum_scatter(
        jnp.dot(attended, output_weight, preferred_element_type=jnp.float32).astype(jnp.bfloat16),
        "mp",
        scatter_dimension=0,
        tiled=True,
    ).astype(jnp.float32)
    inv_two, unit_two, normed_two = norm_parts(middle, feedforward_gain)
    gathered_two = lax.all_gather(normed_two, "mp", axis=0, tiled=True)
    gate = jnp.dot(gathered_two, gate_weight, preferred_element_type=jnp.float32)
    up_rows = jnp.dot(gathered_two, up_weight, preferred_element_type=jnp.float32)

    def gated(gate_in, up_in):
        return jax.nn.gelu(gate_in, approximate=True) * up_in

    hidden_full, gated_pullback = jax.vjp(gated, gate, up_rows)
    hidden = hidden_full.astype(jnp.bfloat16)
    layer_out = middle + lax.psum_scatter(
        jnp.dot(hidden, down_weight, preferred_element_type=jnp.float32).astype(jnp.bfloat16),
        "mp",
        scatter_dimension=0,
        tiled=True,
    ).astype(jnp.float32)
    masked = jnp.where(row_valid[:, None], cotangent, jnp.zeros_like(cotangent))
    grad_rows = lax.all_gather(masked, "mp", axis=0, tiled=True)
    grad_hidden = contract_cols(grad_rows, down_weight)
    down_grad = contract_rows(hidden, grad_rows)
    grad_gate_full, grad_up_full = gated_pullback(grad_hidden)
    grad_gate = grad_gate_full.astype(jnp.bfloat16)
    grad_up = grad_up_full.astype(jnp.bfloat16)
    gate_grad = contract_rows(gathered_two, grad_gate)
    up_grad = contract_rows(gathered_two, grad_up)
    grad_normed_two = lax.psum_scatter(
        (contract_cols(grad_gate, gate_weight) + contract_cols(grad_up, up_weight)).astype(
            jnp.bfloat16
        ),
        "mp",
        scatter_dimension=0,
        tiled=True,
    ).astype(jnp.float32)
    back_two, gain_two = norm_back(grad_normed_two, inv_two, unit_two, feedforward_gain)
    grad_middle = masked.astype(jnp.float32) + back_two
    grad_branch = lax.all_gather(grad_middle.astype(jnp.bfloat16), "mp", axis=0, tiled=True)
    output_grad = contract_rows(attended, grad_branch)
    grad_attended = (
        contract_cols(grad_branch, output_weight)
        .astype(jnp.bfloat16)
        .reshape(seq_len, local_heads, DKV)
    )

    def backward_block(carried, inputs):
        key_sums, value_sums, diag_sums = carried
        first_row, log_total = inputs
        query_block, scores = block_scores(first_row)
        probabilities = jnp.exp(scores - log_total[:, :, None])
        grad_probs = jnp.einsum(
            "qhd,khd->hqk", grad_attended, values, preferred_element_type=jnp.float32
        )
        inner = jnp.sum(probabilities * grad_probs, axis=2, keepdims=True)
        grad_scores = (probabilities * (grad_probs - inner)).astype(jnp.bfloat16)
        grad_query = jnp.einsum(
            "hqk,khd->qhd", grad_scores, key_rows, preferred_element_type=jnp.float32
        )
        key_sums = key_sums + jnp.einsum(
            "hqk,qhd->khd", grad_scores, query_block, preferred_element_type=jnp.float32
        )
        value_sums = value_sums + jnp.einsum(
            "hqk,qhd->khd",
            probabilities.astype(jnp.bfloat16),
            grad_attended,
            preferred_element_type=jnp.float32,
        )
        diag_sums = add_diagonals(diag_sums, grad_scores.astype(jnp.float32), first_row)
        return ((key_sums, value_sums, diag_sums), grad_query.astype(jnp.bfloat16))

    start_state = (
        jnp.zeros((seq_len, local_heads, DKV), jnp.float32),
        jnp.zeros((seq_len, local_heads, DKV), jnp.float32),
        jnp.zeros((local_heads, 2 * seq_len + block_rows), jnp.float32),
    )
    (key_sums, value_sums, diag_sums), query_blocks = lax.scan(
        backward_block, start_state, (block_starts, log_totals)
    )
    grad_joined = jnp.concatenate(
        [
            query_blocks.reshape(seq_len, head_width),
            key_sums.reshape(seq_len, head_width).astype(jnp.bfloat16),
            value_sums.reshape(seq_len, head_width).astype(jnp.bfloat16),
        ],
        axis=1,
    )
    joined_grad = contract_rows(gathered_one, grad_joined)
    query_grad = joined_grad[:, :head_width]
    key_grad = joined_grad[:, head_width : 2 * head_width]
    value_grad = joined_grad[:, 2 * head_width :]
    diagonals = diag_sums[:, block_rows : block_rows + 2 * seq_len - 1]
    bias_grad = jnp.dot(onehot.T, diagonals.T, precision=lax.Precision.HIGHEST)
    grad_normed_one = lax.psum_scatter(
        contract_cols(grad_joined, joined_weight).astype(jnp.bfloat16),
        "mp",
        scatter_dimension=0,
        tiled=True,
    ).astype(jnp.float32)
    back_one, gain_one = norm_back(grad_normed_one, inv_one, unit_one, attention_gain)
    input_grad = grad_middle + back_one
    query_sum, key_sum, value_sum, output_sum, gate_sum, up_sum, down_sum = (
        lax.psum_scatter(query_grad, "dp", scatter_dimension=0, tiled=True),
        lax.psum_scatter(key_grad, "dp", scatter_dimension=0, tiled=True),
        lax.psum_scatter(value_grad, "dp", scatter_dimension=0, tiled=True),
        lax.psum_scatter(output_grad, "dp", scatter_dimension=1, tiled=True),
        lax.psum_scatter(gate_grad, "dp", scatter_dimension=0, tiled=True),
        lax.psum_scatter(up_grad, "dp", scatter_dimension=0, tiled=True),
        lax.psum_scatter(down_grad, "dp", scatter_dimension=1, tiled=True),
    )
    gain_one_sum, gain_two_sum = lax.psum((gain_one, gain_two), ("dp", "mp"))
    bias_total = lax.psum(bias_grad, "dp")
    return (
        layer_out,
        input_grad,
        gain_one_sum,
        query_sum,
        key_sum,
        value_sum,
        output_sum,
        bias_total,
        gain_two_sum,
        gate_sum,
        up_sum,
        down_sum,
    )


def solution(mesh):
    in_specs = (
        P(("dp", "mp"), None),
        P(),
        P(None, "mp"),
        P(None, "mp"),
        P(None, "mp"),
        P("mp", None),
        P(None, "mp"),
        P(),
        P(None, "mp"),
        P(None, "mp"),
        P("mp", None),
        P(("dp", "mp"), None),
        P(),
        P(),
        P(),
    )
    out_specs = (
        P(("dp", "mp"), None),
        P(("dp", "mp"), None),
        P(),
        P("dp", "mp"),
        P("dp", "mp"),
        P("dp", "mp"),
        P("mp", "dp"),
        P(None, "mp"),
        P(),
        P("dp", "mp"),
        P("dp", "mp"),
        P("mp", "dp"),
    )
    return jax.shard_map(shards, mesh=mesh, in_specs=in_specs, out_specs=out_specs, check_vma=False)
```

profile of v0, /device:TPU:0, one launch (start us, length us, event | category | flops | bytes accessed | tf_op | source)
XLA Modules:
  0.0 1238.9 jit_solution(13118240986731563491)
XLA Ops:
  7.3 1.2 constant_dynamic-update-slice_fusion.2
  8.5 1.3 fusion.28
  10.1 2.4 all_gather.12
  14.7 217.0 %gather_fusion = f32[65536,3]{1,0:T(8,128)} fusion(f32[3,511]{0,1:T(8,128)S(1)} %copy.48, s32[65536]{0:T(1024)S(1)} %broadcast_clamp_fusion), kind=kCustom, calls=%fused_computation.clone | custom fusion | bytes 1835008 | tf_op jit(solution)/shard_map/while/body/eval_jaxpr/jit(_take)/gather | solution.py:109
  231.8 19.0 %copy.50 = f32[256,256,3]{0,1,2:T(8,128)S(1)} copy(f32[256,256,3]{2,1,0:T(8,128)} %bitcast.86) | data formatting | bytes 1572864 | tf_op jit(solution)/shard_map/while/body/eval_jaxpr/jit(_take)/gather | solution.py:109
  254.2 1.2 copy.65
  258.0 2.3 all_gather.14
  260.4 6.0 reduce-scatter.23.cloned.1.call-done
  266.4 1.2 copy.66
  268.1 2.7 all_gather.13
  270.8 4.3 fusion.51
  275.1 1.6 fusion.52
  276.7 3.9 multiply_convert_fusion
  280.7 1.6 fusion.53
  282.2 5.6 fusion.55
  287.8 5.4 fusion.56
  293.2 2.5 fusion.3
  295.7 2.3 copy.69
  298.3 6.7 fusion.57
  305.0 675.1 %fusion.46 = (f32[96,1792]{1,0:T(8,128)}, f32[96,1792]{1,0:T(8,128)S(1)}, f32[1792,96]{0,1:T(8,128)S(1)}) fusion(f32[1472,1792]{1,0:T(8,128)} %fusion.55, f32[1472,1792]{1,0:T(8,128)} %fusion.56, f32[1792,1472]{0,1:T(8,128)} %fusion.57), kind=kCustom, calls=%all-reduce-scatter.3 | all-reduce-scatter fusion | flops 8257537 | bytes 33718784
  980.1 1.9 slice.38
  982.0 2.1 collective-permute-start
  984.8 2.5 collective-permute-start.1
  987.4 4.9 convolution_convert_fusion.1
  992.3 2.3 copy.67
  995.4 4.4 collective-permute-start.2
  999.9 5.1 concatenate.18
  1005.0 4.7 concatenate.19
  1009.7 2.1 constant_dynamic-slice_fusion.2
  1013.2 4.7 concatenate.20
  1017.8 1.2 copy.70
  1020.2 2.3 all_gather.15
  1026.1 1.2 copy.71
  1027.6 2.0 constant_dynamic-slice_fusion
  1029.9 1.7 copy.83
  1031.5 1.5 fusion.54
  1033.7 1.9 fusion.47
  1035.6 1.2 copy-done.6
  1036.8 1.6 pad_convert_fusion
  1038.4 4.9 reshape.127
  1043.4 1.7 reduce_sum.101
  1045.1 1.2 copy.68
  1046.6 43.8 %psum.22 = f32[32,3]{0,1:T(4,128)} all-reduce(f32[32,3]{0,1:T(4,128)S(1)} %fusion.34), channel_id=1, replica_groups=mesh['dp'=16,'mp'=2] {'dp'}, use_global_device_ids=true, to_apply=%region_19.21 | all-reduce | flops 96 | bytes 768 | tf_op jit(solution)/shard_map/psum | solution.py:240
  1090.5 1.2 copy.72
  1092.2 38.0 %all-reduce.12 = (f32[1472]{0:T(1024)}, f32[1472]{0:T(1024)}) all-reduce(f32[1472]{0:T(1024)S(1)} %get-tuple-element.117, f32[1472]{0:T(1024)S(1)} %get-tuple-element.115), channel_id=1, replica_groups=mesh['dp'=16,'mp'=2] {'dp','mp'}, use_global_device_ids=true, to_apply=%region_13.15 | all-reduce | flops 2944 | bytes 23552 | tf_op jit(solution)/shard_map/psum | solution.py:239
  1130.2 1.7 fusion.20
  1131.9 94.4 %all-reduce.17.cloned.1.call-done = (f32[1472,192]{0,1:T(8,128)}, f32[1472,192]{0,1:T(8,128)}, f32[1472,192]{0,1:T(8,128)}, f32[192,1472]{1,0:T(8,128)}) async-done(((f32[1472,192]{0,1:T(8,128)}, f32[1472,192]{0,1:T(8,128)}, f32[1472,192]{0,1:T(8,128)}, f32[192,1472]{1,0:T(8,128)}), (f32[1472,192]{0,1:T(8,128)}, f32[1472,192]{0,1:T(8,128)}, f32[1472,192]{0,1:T(8,128)}, ...) | async-done | bytes 4522000
  1230.7 1.7 constant_dynamic-slice_fusion.3
  (146 shorter events, 22.0 us)
Async XLA Ops:
  7.2 246.5 %copy-start = (bf16[192,1472]{1,0:T(8,128)(2,1)S(1)}, bf16[192,1472]{1,0:T(8,128)(2,1)}, u32[]{:S(2)}) copy-start(bf16[192,1472]{1,0:T(8,128)(2,1)} %param.22) | copy-start | bytes 1695748
  7.2 2.6 copy-start.1
  7.2 2.6 copy-start.27
  7.2 5.3 copy-start.20
  7.2 259.1 %reduce-scatter.23.cloned.1.call-start = ((), (), s32[]{:S(2)}) async-start(), calls=%async_computation.4 | async-start | bytes 1179648
  8.5 4.0 copy-start.21
  12.5 0.9 copy-start.2
  12.6 1.4 copy-start.24
  12.6 1.4 copy-start.31
  12.6 1.4 copy-start.32
  14.0 238.2 %copy-start.14 = (bf16[256,192]{0,1:T(8,128)(2,1)}, bf16[256,192]{0,1:T(8,128)(2,1)S(1)}, u32[]{:S(2)}) copy-start(bf16[256,192]{0,1:T(8,128)(2,1)S(1)} %get-tuple-element.139) | copy-start | bytes 294916
  14.0 238.2 %copy-start.16 = (bf16[256,192]{0,1:T(8,128)(2,1)}, bf16[256,192]{0,1:T(8,128)(2,1)S(1)}, u32[]{:S(2)}) copy-start(bf16[256,192]{0,1:T(8,128)(2,1)S(1)} %get-tuple-element.140) | copy-start | bytes 294916
  14.1 238.8 %copy-start.18 = (bf16[256,192]{0,1:T(8,128)(2,1)}, bf16[256,192]{0,1:T(8,128)(2,1)S(1)}, u32[]{:S(2)}) copy-start(bf16[256,192]{0,1:T(8,128)(2,1)S(1)} %get-tuple-element.141) | copy-start | bytes 294916
  231.8 19.2 %copy-start.29 = (s32[16]{0:T(128)S(1)}, s32[16]{0:T(128)}, u32[]{:S(2)}) copy-start(s32[16]{0:T(128)} %param.29) | copy-start | bytes 196
  231.8 19.2 %copy-start.30 = (s32[16]{0:T(128)S(1)}, s32[16]{0:T(128)}, u32[]{:S(2)}) copy-start(s32[16]{0:T(128)} %param.30) | copy-start | bytes 196
  253.1 0.7 copy-start.12
  253.7 1.7 copy-start.28
  253.7 4.3 copy-start.7
  255.3 12.5 %copy-start.26 = (f32[1472]{0:T(1024)S(1)}, f32[1472]{0:T(1024)}, u32[]{:S(2)}) copy-start(f32[1472]{0:T(1024)} %param.24) | copy-start | bytes 17668
  255.4 762.5 %reduce-scatter.27.cloned.1.call-start = ((), (), s32[]{:S(2)}) async-start(), calls=%async_computation.6 | async-start | bytes 1179648
  268.1 6.9 slice-start.2
  270.8 4.3 slice-start.3
  270.8 5.9 slice-start.4
  275.1 1.7 slice-start.5
  275.1 5.6 slice-start
  276.7 3.9 slice-start.1
  298.1 747.1 %reduce-scatter.25.cloned.1.call-start = ((), (), s32[]{:S(2)}) async-start(), calls=%async_computation.5 | async-start | bytes 1179648
  980.1 7.3 copy-start.11
  982.0 17.9 %collective-permute-start = (f32[60,1792]{1,0:T(8,128)}, f32[60,1792]{1,0:T(8,128)}, u32[]{:S(2)}, u32[]{:S(2)}) collective-permute-start(f32[60,1792]{1,0:T(8,128)} %slice.38), channel_id=1, source_target_pairs={{0,2},{2,4},{4,6},{6,8},{8,10},{10,12},{12,14},{14,16},{16,18},{18... | collective-permute-start | bytes 1290248
  984.8 20.2 %collective-permute-start.1 = (f32[60,1792]{1,0:T(8,128)}, f32[60,1792]{1,0:T(8,128)}, u32[]{:S(2)}, u32[]{:S(2)}) collective-permute-start(f32[60,1792]{1,0:T(8,128)} %slice.39), channel_id=1, source_target_pairs={{0,2},{2,4},{4,6},{6,8},{8,10},{10,12},{12,14},{14,16},{16,18},{18... | collective-permute-start | bytes 1290248
  995.4 17.8 %collective-permute-start.2 = (f32[1792,60]{0,1:T(8,128)}, f32[1792,60]{0,1:T(8,128)}, u32[]{:S(2)}, u32[]{:S(2)}) collective-permute-start(f32[1792,60]{0,1:T(8,128)} %slice.40), channel_id=1, source_target_pairs={{0,2},{2,4},{4,6},{6,8},{8,10},{10,12},{12,14},{14,16},{16,18},{18... | collective-permute-start | bytes 1290248
  999.8 90.6 %reduce-scatter.29.cloned.1.call-start = ((), (), s32[]{:S(2)}) async-start(), calls=%async_computation.7 | async-start | bytes 1179648
  1009.7 2.1 copy-start.10
  1012.7 7.1 copy-start.8
  1019.1 0.7 copy-start.4
  1019.8 3.0 copy-start.19
  1022.9 0.9 copy-start.17
  1022.9 1.1 copy-start.15
  1023.2 1.9 copy-start.25
  1024.5 0.7 copy-start.22
  1027.3 199.1 %all-reduce.17.cloned.1.call-start = ((), (), s32[]{:S(2)}) async-start(), calls=%async_computation.8 | async-start | bytes 9437184
  1029.6 1.9 copy-start.13
  1029.8 3.2 copy-start.3
  1029.9 3.2 copy-start.23
  1035.6 1.2 copy-start.6
  1043.4 86.9 %copy-start.5 = (bf16[128,1472]{0,1:T(8,128)(2,1)S(1)}, bf16[128,1472]{0,1:T(8,128)(2,1)}, u32[]{:S(2)}) copy-start(bf16[128,1472]{0,1:T(8,128)(2,1)} %copy-done.4) | copy-start | bytes 1130500
  1043.4 86.9 %copy-start.9 = (bf16[128,1472]{0,1:T(8,128)(2,1)S(1)}, bf16[128,1472]{0,1:T(8,128)(2,1)}, u32[]{:S(2)}) copy-start(bf16[128,1472]{0,1:T(8,128)(2,1)} %param.28) | copy-start | bytes 1130500
Sparse Core Ops, SparseCore 0:
  255.5 10.8 reduce-scatter.22
  298.2 9.3 reduce-scatter.26
  1000.0 6.6 reduce-scatter.24
  1027.4 9.9 reduce-scatter.28
  1043.2 183.0 all-reduce.16
where the time goes:
time: 1240 us
  blocking collectives  767 us (62%)
  local copies, waits for them, and re-layouts  292 us (24%)
  waiting for transfers between devices  101 us (8%)
  matrix products  43.2 us (3%)
  between operations  15.7 us (1%)
    unnamed x1, blocking collectives  675 us
    gather x2, local copies, waits for them, and re-layouts, block_scores(): bias_rows = jnp.take(bias_by_offset, offsets, axis=1)  236 us
    unnamed x13, waiting for transfers between devices  101 us
    unnamed x108, local copies, waits for them, and re-layouts  48.7 us
    psum x1, blocking collectives, shards(): bias_total = lax.psum(bias_grad, 'dp')  43.8 us
    psum x1, blocking collectives, shards(): gain_one_sum, gain_two_sum = lax.psum((gain_one, gain_two), ('dp', 'mp'))  38 us
  transfers between devices with their start and end apart: 8, of which 3 were waited for; matrix products, arithmetic and copies ran while one was open for 60% of the time, Pallas kernels for 0%

commit v1 on v0

v1 whole, which is shorter than its diff:
```python
import functools
import math

import jax
import jax.numpy as jnp
from jax import lax
from jax.experimental import pallas as pl
from jax.experimental.pallas import tpu as pltpu
from jax.sharding import PartitionSpec as P

DKV = 64
CW = 256
EPS = 1e-06
LAG = 3
GAP = 2
SLOTS = 3
BF = jnp.bfloat16
F32 = jnp.float32
MESH = pl.DeviceIdType.MESH
GELU_C = math.sqrt(2.0 / math.pi)


def dot(left, right):
    return lax.dot_general(left, right, (((1,), (0,)), ((), ())), preferred_element_type=F32)


def dot_nt(left, right):
    return lax.dot_general(left, right, (((1,), (1,)), ((), ())), preferred_element_type=F32)


def dot_tn(left, right):
    return lax.dot_general(left, right, (((0,), (0,)), ((), ())), preferred_element_type=F32)


def column_blocks(width, step=256):
    return [(begin, min(step, width - begin)) for begin in range(0, width, step)]


class Sizes:
    def __init__(self, dp, local_rows, width, head_width, hidden, buckets):
        self.dp = dp
        self.bits = dp.bit_length() - 1
        self.local_rows = local_rows
        self.seq = 2 * local_rows
        self.width = width
        self.head_width = head_width
        self.heads = head_width // DKV
        self.hidden = hidden
        self.buckets = buckets
        self.shard = width // dp
        self.shard_pad = -(-self.shard // 16) * 16
        self.quarter = self.shard_pad * dp // 4
        self.ff_chunks = hidden // CW
        self.ff_total = 3 * self.ff_chunks
        self.chunks = self.ff_total + 4 * head_width // CW
        self.stage_rows = [self.quarter >> k for k in range(self.bits - 1)]
        self.stages = len(self.stage_rows)
        self.wide = -(-width // 256) * 256


def layer_kernel(
    cfg,
    hidden_hbm,
    gain_one,
    wq_hbm,
    wk_hbm,
    wv_hbm,
    wo_hbm,
    position_bias,
    gain_two,
    wg_hbm,
    wu_hbm,
    wd_hbm,
    cot_hbm,
    lengths,
    groups,
    bucket_ids,
    layer_out,
    input_grad,
    small_out,
    final_out,
    hid,
    cot,
    wqkv,
    wo,
    wg,
    wu,
    wd,
    normed_one,
    normed_two,
    middle,
    qkv,
    probs,
    attended,
    trans,
    left_own,
    left_in,
    right_own,
    right_in,
    out_acc,
    grad_acc,
    grad_send,
    grad_in,
    part_send,
    part_in,
    back_send,
    back_in,
    grad_branch,
    grad_qkv,
    small,
    small_in,
    *rest,
):
    stages = cfg.stages
    stage_own = rest[:stages]
    stage_send = rest[stages : 2 * stages]
    stage_in = rest[2 * stages : 3 * stages]
    (
        load_sem,
        weight_sem,
        pair_send_sem,
        pair_recv_sem,
        left_send_sem,
        left_recv_sem,
        right_send_sem,
        right_recv_sem,
        stage_send_sem,
        stage_recv_sem,
        small_send_sem,
        small_recv_sem,
    ) = rest[3 * stages :]

    seq, rows, width, hw, heads = cfg.seq, cfg.local_rows, cfg.width, cfg.head_width, cfg.heads
    me = lax.axis_index("dp")
    core = lax.axis_index("mp")
    bit = [lax.rem(lax.div(me, 1 << k), 2) for k in range(cfg.bits)]
    peer = [me + (1 - 2 * bit[k]) * (1 << k) for k in range(cfg.bits)]
    sibling = (me, 1 - core)
    own_begin = pl.multiple_of(core * rows, rows)
    other_begin = pl.multiple_of((1 - core) * rows, rows)
    own_rows = pl.ds(own_begin, rows)
    other_rows = pl.ds(other_begin, rows)

    def send(src, dst, send_sem, recv_sem, target):
        return pltpu.make_async_remote_copy(
            src_ref=src,
            dst_ref=dst,
            send_sem=send_sem,
            recv_sem=recv_sem,
            device_id=target,
            device_id_type=MESH,
        )

    head_rows = pl.ds(pl.multiple_of(core * hw, hw), hw)
    loads = [
        pltpu.make_async_copy(hidden_hbm, hid.at[own_rows], load_sem.at[0]),
        pltpu.make_async_copy(cot_hbm, cot.at[own_rows], load_sem.at[1]),
        pltpu.make_async_copy(wq_hbm, wqkv.at[0], load_sem.at[2]),
        pltpu.make_async_copy(wk_hbm, wqkv.at[1], load_sem.at[3]),
        pltpu.make_async_copy(wv_hbm, wqkv.at[2], load_sem.at[4]),
        pltpu.make_async_copy(wo_hbm, wo.at[core], load_sem.at[5]),
    ]
    for load in loads:
        load.start()

    def weight_loads(chunk, slot):
        columns = pl.ds(pl.multiple_of(chunk * CW, CW), CW)
        return [
            pltpu.make_async_copy(wg_hbm.at[:, columns], wg.at[slot], weight_sem.at[slot, 0]),
            pltpu.make_async_copy(wu_hbm.at[:, columns], wu.at[slot], weight_sem.at[slot, 1]),
            pltpu.make_async_copy(wd_hbm.at[columns, :], wd.at[slot], weight_sem.at[slot, 2]),
        ]

    barrier = pltpu.get_barrier_semaphore()
    pl.semaphore_signal(barrier, inc=1, device_id=sibling, device_id_type=MESH)
    for k in range(cfg.bits):
        pl.semaphore_signal(barrier, inc=1, device_id=(peer[k], core), device_id_type=MESH)
    pl.semaphore_wait(barrier, cfg.bits + 1)

    pair_hid = send(
        hidden_hbm, hid.at[own_rows], pair_send_sem.at[0], pair_recv_sem.at[0], sibling
    )
    pair_cot = send(cot_hbm, cot.at[own_rows], pair_send_sem.at[1], pair_recv_sem.at[1], sibling)
    pair_wo = send(wo_hbm, wo.at[core], pair_send_sem.at[2], pair_recv_sem.at[2], sibling)
    pair_hid.start()
    pair_cot.start()
    pair_wo.start()
    pair_att = send(
        attended.at[core], attended.at[core], pair_send_sem.at[3], pair_recv_sem.at[3], sibling
    )
    pair_grad = send(grad_send, grad_in, pair_send_sem.at[4], pair_recv_sem.at[4], sibling)
    pair_part = send(part_send, part_in, pair_send_sem.at[5], pair_recv_sem.at[5], sibling)
    pair_back = send(back_send, back_in, pair_send_sem.at[6], pair_recv_sem.at[6], sibling)

    for slot in range(2):
        for load in weight_loads(slot, slot):
            load.start()

    group_len = jnp.int32(0)
    for item in range(lengths.shape[0]):
        group_len = group_len + jnp.where(groups[item] == me, lengths[item], 0)

    left_axis = (0, 1, 1, 1)

    def build_left(source, which):
        for begin, size in column_blocks(width, 128):
            trans[begin : begin + size, :] = jnp.transpose(
                source[:, begin : begin + size].astype(F32)
            )
        first = left_axis[which]
        for index in range(cfg.dp):
            low = (index & 1, (index >> 1) & 1)
            place = 0
            for k in range(2, cfg.bits):
                place = 2 * place + ((index >> k) & 1)
            block = trans[index * cfg.shard : index * cfg.shard + cfg.shard_pad, :]
            left_own[
                which,
                low[first],
                low[1 - first],
                place * cfg.shard_pad : (place + 1) * cfg.shard_pad,
                :,
            ] = block.astype(BF)

    def left_copy(which):
        first = left_axis[which]
        return send(
            left_own.at[which, 1 - bit[first]],
            left_in.at[which],
            left_send_sem.at[which],
            left_recv_sem.at[which],
            (peer[first], core),
        )

    def right_copy(chunk, first):
        return send(
            right_own.at[chunk],
            right_in.at[chunk],
            right_send_sem.at[chunk],
            right_recv_sem.at[chunk],
            (peer[first], core),
        )

    tail = trans.shape[0] - width
    trans[width:, :] = jnp.zeros((tail, seq), F32)

    loads[0].wait()
    pair_hid.wait()

    def norm_one_rows(step, carry):
        block = pl.ds(pl.multiple_of(step * 32, 32), 32)
        x = hid[block, :].astype(F32)
        inv = lax.rsqrt(jnp.mean(x * x, axis=1, keepdims=True) + EPS)
        normed_one[block, :] = (x * inv * gain_one[...]).astype(BF)
        return carry

    lax.fori_loop(0, seq // 32, norm_one_rows, 0)

    for part in range(3):
        loads[2 + part].wait()
        qkv[part] = dot(normed_one[...], wqkv[part]).astype(BF)

    key_valid = lax.broadcasted_iota(jnp.int32, (seq, seq), 1) < group_len
    ids = bucket_ids[...]
    mixed = []
    for head in range(heads):
        lanes = slice(head * DKV, (head + 1) * DKV)
        by_offset = jnp.zeros(ids.shape, F32)
        for bucket in range(cfg.buckets):
            by_offset = jnp.where(ids == bucket, position_bias[bucket, head], by_offset)
        bias = pltpu.roll(
            jnp.broadcast_to(by_offset, (seq, 2 * seq)),
            seq + 1,
            1,
            stride=1,
            stride_axis=0,
        )[:, :seq]
        scores = dot_nt(qkv[0, :, lanes], qkv[1, :, lanes]) + bias
        scores = jnp.where(key_valid, scores, -1e30)
        exps = jnp.exp(scores - jnp.max(scores, axis=1, keepdims=True))
        prob = exps / jnp.sum(exps, axis=1, keepdims=True)
        probs[head] = prob
        mixed.append(dot(prob.astype(BF), qkv[2, :, lanes]).astype(BF))
    own_attended = jnp.concatenate(mixed, axis=1)
    attended[core] = own_attended
    pair_att.start()

    loads[1].wait()
    pair_cot.wait()

    def mask_rows(step, carry):
        begin = pl.multiple_of(step * 32, 32)
        block = pl.ds(begin, 32)
        keep = begin + lax.broadcasted_iota(jnp.int32, (32, width), 0) < group_len
        cot[block, :] = jnp.where(keep, cot[block, :].astype(F32), 0.0).astype(BF)
        return carry

    lax.fori_loop(0, seq // 32, mask_rows, 0)
    build_left(cot, 0)
    left_copy(0).start()
    build_left(normed_one, 2)
    left_copy(2).start()

    loads[5].wait()
    pair_wo.wait()
    pair_att.wait()
    for begin, size in column_blocks(width):
        columns = slice(begin, begin + size)
        middle[:, columns] = (
            hid[:, columns].astype(F32)
            + dot(attended[0], wo[0, :, columns])
            + dot(attended[1], wo[1, :, columns])
        )

    def norm_two_rows(step, carry):
        block = pl.ds(pl.multiple_of(step * 32, 32), 32)
        x = middle[block, :]
        inv = lax.rsqrt(jnp.mean(x * x, axis=1, keepdims=True) + EPS)
        normed_two[block, :] = (x * inv * gain_two[...]).astype(BF)
        out_acc[block, :] = jnp.zeros((32, width), F32)
        grad_acc[block, :] = jnp.zeros((32, width), F32)
        return carry

    lax.fori_loop(0, seq // 32, norm_two_rows, 0)
    build_left(normed_two, 1)
    left_copy(1).start()
    small[...] = jnp.zeros_like(small)

    def feed_forward(chunk):
        slot = lax.rem(chunk, 2)
        for load in weight_loads(chunk, slot):
            load.wait()
        normed = normed_two[...]
        gate = dot(normed, wg[slot])
        up = dot(normed, wu[slot])
        grad_hidden = dot_nt(cot[...], wd[slot])
        square = gate * gate
        tanh = jnp.tanh(GELU_C * (gate + 0.044715 * (square * gate)))
        half = 0.5 * (1.0 + tanh)
        gelu = gate * half
        slope = half + (0.5 * GELU_C) * gate * (1.0 - tanh * tanh) * (
            1.0 + (3 * 0.044715) * square
        )
        hidden = (gelu * up).astype(BF)
        grad_gate = (grad_hidden * up * slope).astype(BF)
        grad_up = (grad_hidden * gelu).astype(BF)
        base = 3 * chunk
        right_own[base] = hidden
        right_own[base + 1] = grad_gate
        right_own[base + 2] = grad_up
        right_copy(base, 0).start()
        right_copy(base + 1, 1).start()
        right_copy(base + 2, 1).start()
        for begin, size in column_blocks(width):
            columns = slice(begin, begin + size)
            out_acc[:, columns] += dot(hidden, wd[slot, :, columns])
            grad_acc[:, columns] += dot_nt(grad_gate, wg[slot, columns, :]) + dot_nt(
                grad_up, wu[slot, columns, :]
            )

        @pl.when(chunk < cfg.ff_chunks - 2)
        def _():
            for load in weight_loads(chunk + 2, slot):
                load.start()

    def exchange_sums():
        grad_send[...] = grad_acc[...].astype(BF)
        pair_grad.start()
        part_send[...] = out_acc[other_rows, :].astype(BF)
        pair_part.start()

    def norm_two_back():
        pair_grad.wait()
        gain = gain_two[...]

        def back_rows(step, carry):
            block = pl.ds(pl.multiple_of(step * 32, 32), 32)
            grad = grad_acc[block, :] + grad_in[block, :].astype(F32)
            x = middle[block, :]
            inv = lax.rsqrt(jnp.mean(x * x, axis=1, keepdims=True) + EPS)
            unit = x * inv
            scaled = grad * gain
            inner = jnp.mean(scaled * unit, axis=1, keepdims=True)
            total = cot[block, :].astype(F32) + inv * (scaled - unit * inner)
            grad_acc[block, :] = total
            grad_branch[block, :] = total.astype(BF)
            mine = lax.div(step * 32, rows) == core
            small[1:2, :width] += jnp.where(
                mine, jnp.sum(grad * unit, axis=0, keepdims=True), 0.0
            )
            return carry

        lax.fori_loop(0, seq // 32, back_rows, 0)
        build_left(grad_branch, 3)
        left_copy(3).start()

    def attention_back():
        grad_att = dot_nt(grad_branch[...], wo[core]).astype(BF)
        flip = (
            lax.broadcasted_iota(jnp.int32, (seq, seq), 0)
            + lax.broadcasted_iota(jnp.int32, (seq, seq), 1)
            == seq - 1
        ).astype(BF)
        parts = [[], [], []]
        for head in range(heads):
            lanes = slice(head * DKV, (head + 1) * DKV)
            grad_mixed = grad_att[:, lanes]
            prob = probs[head]
            grad_probs = dot_nt(grad_mixed, qkv[2, :, lanes])
            inner = jnp.sum(prob * grad_probs, axis=1, keepdims=True)
            grad_scores = (prob * (grad_probs - inner)).astype(BF)
            parts[0].append(dot(grad_scores, qkv[1, :, lanes]).astype(BF))
            parts[1].append(dot_tn(grad_scores, qkv[0, :, lanes]).astype(BF))
            parts[2].append(dot_tn(prob.astype(BF), grad_mixed).astype(BF))
            flipped = jnp.concatenate(
                [dot(flip, grad_scores), jnp.zeros((seq, seq), F32)], axis=1
            )
            skewed = pltpu.roll(flipped, 0, 1, stride=1, stride_axis=0)
            small[2 + head : 3 + head, : 2 * seq] = jnp.sum(skewed, axis=0, keepdims=True)
        for part in range(3):
            grad_qkv[part] = jnp.concatenate(parts[part], axis=1)
        joined = jnp.concatenate(
            parts[0] + parts[1] + parts[2] + [attended[core]], axis=1
        )
        for index in range(cfg.chunks - cfg.ff_total):
            chunk = cfg.ff_total + index
            right_own[chunk] = joined[:, index * CW : (index + 1) * CW]
            right_copy(chunk, 1).start()

    def norm_one_sums():
        for begin, size in column_blocks(width):
            columns = slice(begin, begin + size)
            back_send[:, columns] = sum(
                dot_nt(grad_qkv[part, other_rows, :], wqkv[part, columns, :]) for part in range(3)
            ).astype(BF)
        pair_back.start()
        for begin, size in column_blocks(width):
            columns = slice(begin, begin + size)
            input_grad[:, columns] = sum(
                dot_nt(grad_qkv[part, own_rows, :], wqkv[part, columns, :]) for part in range(3)
            )

    def small_copy(k):
        target = sibling if k == cfg.bits else (peer[k], core)
        return send(
            small, small_in.at[k], small_send_sem.at[k], small_recv_sem.at[k], target
        )

    def finish_rows():
        pair_part.wait()
        pair_back.wait()
        gain = gain_one[...]

        def last_rows(step, carry):
            block = pl.ds(pl.multiple_of(step * 32, 32), 32)
            whole = pl.ds(pl.multiple_of(own_begin + step * 32, 32), 32)
            grad = input_grad[block, :] + back_in[block, :].astype(F32)
            x = hid[whole, :].astype(F32)
            inv = lax.rsqrt(jnp.mean(x * x, axis=1, keepdims=True) + EPS)
            unit = x * inv
            scaled = grad * gain
            inner = jnp.mean(scaled * unit, axis=1, keepdims=True)
            input_grad[block, :] = grad_acc[whole, :] + inv * (scaled - unit * inner)
            layer_out[block, :] = (
                middle[whole, :] + out_acc[whole, :] + part_in[block, :].astype(F32)
            )
            small[0:1, :width] += jnp.sum(grad * unit, axis=0, keepdims=True)
            return carry

        lax.fori_loop(0, rows // 32, last_rows, 0)
        small_copy(0).start()

    def small_stage(k):
        small_copy(k).wait()
        if k == cfg.bits:
            row = lax.broadcasted_iota(jnp.int32, small.shape, 0)
            small_out[...] = small[...] + jnp.where(row < 2, small_in[k], 0.0)
        else:
            small[...] = small[...] + small_in[k]
            small_copy(k + 1).start()

    def chunk_kind(chunk):
        tail_part = lax.div(chunk, cfg.ff_total)
        kind = lax.rem(chunk, 3)
        which = (1 - tail_part) * lax.div(kind + 1, 2) + 2 * tail_part
        y_first = 1 - lax.div(2 - which, 2)
        return which, y_first

    def stage_copy(k, chunk, target):
        slot = lax.rem(chunk, SLOTS)
        return send(
            stage_send[k].at[slot],
            stage_in[k].at[chunk],
            stage_send_sem.at[k, slot],
            stage_recv_sem.at[k, chunk],
            (target, core),
        )

    def stage_target(k, chunk):
        if k > 0:
            return peer[k + 1]
        y_first = chunk_kind(chunk)[1]
        return y_first * peer[0] + (1 - y_first) * peer[1]

    def form(chunk):
        which, y_first = chunk_kind(chunk)
        slot = lax.rem(chunk, SLOTS)
        first_bit = y_first * bit[1] + (1 - y_first) * bit[0]
        second_bit = y_first * bit[0] + (1 - y_first) * bit[1]

        @pl.when(chunk == 0)
        def _():
            left_copy(0).wait()

        @pl.when(chunk == 1)
        def _():
            left_copy(1).wait()

        @pl.when(chunk == cfg.ff_total)
        def _():
            left_copy(2).wait()

        right_copy(chunk, 0).wait()

        def product(left, quarter):
            return dot(left_own[left, first_bit, quarter], right_own[chunk]) + dot(
                left_in[left, quarter], right_in[chunk]
            )

        @pl.when(chunk < cfg.chunks - 1)
        def _():
            stage_send[0][slot] = product(which, 1 - second_bit).astype(BF)
            stage_copy(0, chunk, stage_target(0, chunk)).start()
            stage_own[0][slot] = product(which, second_bit)

        @pl.when(chunk == cfg.chunks - 1)
        def _():
            left_copy(3).wait()
            split = lax.broadcasted_iota(jnp.int32, (cfg.quarter, CW), 1) < CW - hw

            def both(quarter):
                return jnp.where(split, product(2, quarter), product(3, quarter))

            stage_send[0][slot] = both(1 - second_bit).astype(BF)
            stage_copy(0, chunk, stage_target(0, chunk)).start()
            stage_own[0][slot] = both(second_bit)

    def halve(k, chunk):
        slot = lax.rem(chunk, SLOTS)
        stage_copy(k - 1, chunk, stage_target(k - 1, chunk)).wait()
        if k == stages:
            final_out[chunk] = stage_own[k - 1][slot] + stage_in[k - 1][chunk].astype(F32)
            return
        half = cfg.stage_rows[k]
        mine = bit[k + 1]

        def total(which):
            part = pl.ds(pl.multiple_of(which * half, 16), half)
            return stage_own[k - 1][slot, part, :] + stage_in[k - 1][chunk, part, :].astype(F32)

        stage_send[k][slot] = total(1 - mine).astype(BF)
        stage_copy(k, chunk, stage_target(k, chunk)).start()
        stage_own[k][slot] = total(mine)

    last_ff = 3 * (cfg.ff_chunks - 1)
    pieces = [exchange_sums, norm_two_back, attention_back, norm_one_sums, finish_rows]
    pieces += [functools.partial(small_stage, k) for k in range(cfg.bits + 1)]
    ticks = max(LAG + cfg.chunks + GAP * stages, last_ff + len(pieces))

    def tick(t, carry):
        for k in range(stages, 0, -1):
            chunk = t - LAG - GAP * k

            @pl.when(jnp.logical_and(chunk >= 0, chunk < cfg.chunks))
            def _(k=k, chunk=chunk):
                halve(k, chunk)

        new = t - LAG

        @pl.when(jnp.logical_and(new >= 0, new < cfg.chunks))
        def _():
            form(new)

        @pl.when(jnp.logical_and(lax.rem(t, 3) == 0, t <= last_ff))
        def _():
            feed_forward(lax.div(t, 3))

        for index, piece in enumerate(pieces):

            @pl.when(t == last_ff + index)
            def _(piece=piece):
                piece()

        return carry

    lax.fori_loop(0, ticks, tick, 0)


def shards(
    mesh,
    hidden_in,
    attention_gain,
    query_weight,
    key_weight,
    value_weight,
    output_weight,
    position_bias,
    feedforward_gain,
    gate_weight,
    up_weight,
    down_weight,
    cotangent,
    item_lengths,
    item_group,
    bucket_ids,
):
    rows, width = hidden_in.shape
    head_width = query_weight.shape[1]
    hidden = gate_weight.shape[1]
    buckets = position_bias.shape[0]
    cfg = Sizes(mesh.shape["dp"], rows, width, head_width, hidden, buckets)
    seq, stages = cfg.seq, cfg.stages
    any_spec = pl.BlockSpec(memory_space=pl.ANY)
    vmem = pl.BlockSpec(memory_space=pltpu.VMEM)
    smem = pl.BlockSpec(memory_space=pltpu.SMEM)
    small_shape = (8, cfg.wide)
    scratch = [
        pltpu.VMEM((seq, width), BF),
        pltpu.VMEM((seq, width), BF),
        pltpu.VMEM((3, width, head_width), BF),
        pltpu.VMEM((2, head_width, width), BF),
        pltpu.VMEM((2, width, CW), BF),
        pltpu.VMEM((2, width, CW), BF),
        pltpu.VMEM((2, CW, width), BF),
        pltpu.VMEM((seq, width), BF),
        pltpu.VMEM((seq, width), BF),
        pltpu.VMEM((seq, width), F32),
        pltpu.VMEM((3, seq, head_width), BF),
        pltpu.VMEM((cfg.heads, seq, seq), F32),
        pltpu.VMEM((2, seq, head_width), BF),
        pltpu.VMEM((width + cfg.shard_pad, seq), F32),
        pltpu.VMEM((4, 2, 2, cfg.quarter, seq), BF),
        pltpu.VMEM((4, 2, cfg.quarter, seq), BF),
        pltpu.VMEM((cfg.chunks, seq, CW), BF),
        pltpu.VMEM((cfg.chunks, seq, CW), BF),
        pltpu.VMEM((seq, width), F32),
        pltpu.VMEM((seq, width), F32),
        pltpu.VMEM((seq, width), BF),
        pltpu.VMEM((seq, width), BF),
        pltpu.VMEM((rows, width), BF),
        pltpu.VMEM((rows, width), BF),
        pltpu.VMEM((rows, width), BF),
        pltpu.VMEM((rows, width), BF),
        pltpu.VMEM((seq, width), BF),
        pltpu.VMEM((3, seq, head_width), BF),
        pltpu.VMEM(small_shape, F32),
        pltpu.VMEM((cfg.bits + 1,) + small_shape, F32),
    ]
    scratch += [pltpu.VMEM((SLOTS, size, CW), F32) for size in cfg.stage_rows]
    scratch += [pltpu.VMEM((SLOTS, size, CW), BF) for size in cfg.stage_rows]
    scratch += [pltpu.VMEM((cfg.chunks, size, CW), BF) for size in cfg.stage_rows]
    dma = pltpu.SemaphoreType.DMA
    scratch += [
        dma((6,)),
        dma((2, 3)),
        dma((7,)),
        dma((7,)),
        dma((4,)),
        dma((4,)),
        dma((cfg.chunks,)),
        dma((cfg.chunks,)),
        dma((stages, SLOTS)),
        dma((stages, cfg.chunks)),
        dma((cfg.bits + 1,)),
        dma((cfg.bits + 1,)),
    ]
    padded_ids = jnp.pad(bucket_ids, (0, 2 * seq - bucket_ids.shape[0]), constant_values=-1)
    layer_out, input_grad, small_sum, final = pl.pallas_call(
        functools.partial(layer_kernel, cfg),
        out_shape=[
            jax.ShapeDtypeStruct((rows, width), F32),
            jax.ShapeDtypeStruct((rows, width), F32),
            jax.ShapeDtypeStruct(small_shape, F32),
            jax.ShapeDtypeStruct((cfg.chunks, cfg.shard_pad, CW), F32),
        ],
        in_specs=[
            any_spec,
            vmem,
            any_spec,
            any_spec,
            any_spec,
            any_spec,
            smem,
            vmem,
            any_spec,
            any_spec,
            any_spec,
            any_spec,
            smem,
            smem,
            vmem,
        ],
        out_specs=[vmem, vmem, vmem, vmem],
        scratch_shapes=scratch,
        compiler_params=pltpu.CompilerParams(
            collective_id=0, has_side_effects=True, vmem_limit_bytes=60 * 1024 * 1024
        ),
        cost_estimate=pl.CostEstimate(
            flops=14 * 10**9, bytes_accessed=24 * 10**6, transcendentals=10**6
        ),
    )(
        hidden_in,
        attention_gain.reshape(1, width),
        query_weight,
        key_weight,
        value_weight,
        output_weight,
        position_bias,
        feedforward_gain.reshape(1, width),
        gate_weight,
        up_weight,
        down_weight,
        cotangent,
        item_lengths,
        item_group,
        padded_ids.reshape(1, -1),
    )

    ff = cfg.ff_total
    shard = cfg.shard

    def joined(first):
        part = final[first:ff:3, :shard, :]
        return jnp.transpose(part, (1, 0, 2)).reshape(shard, hidden)

    down_sum = jnp.transpose(final[0:ff:3, :shard, :], (0, 2, 1)).reshape(hidden, shard)
    attention = jnp.transpose(final[ff:, :shard, :], (1, 0, 2)).reshape(shard, 4 * head_width)
    query_sum, key_sum, value_sum = (
        attention[:, part * head_width : (part + 1) * head_width] for part in range(3)
    )
    output_sum = attention[:, 3 * head_width :].T
    onehot = (
        bucket_ids[None, :] == jnp.arange(buckets, dtype=jnp.int32)[:, None]
    ).astype(F32)
    diagonals = small_sum[2 : 2 + cfg.heads, : bucket_ids.shape[0]]
    bias_total = lax.dot_general(
        onehot, diagonals, (((1,), (1,)), ((), ())), precision=lax.Precision.HIGHEST
    )
    return (
        layer_out,
        input_grad,
        small_sum[0, :width],
        query_sum,
        key_sum,
        value_sum,
        output_sum,
        bias_total,
        small_sum[1, :width],
        joined(1),
        joined(2),
        down_sum,
    )


def solution(mesh):
    in_specs = (
        P(("dp", "mp"), None),
        P(),
        P(None, "mp"),
        P(None, "mp"),
        P(None, "mp"),
        P("mp", None),
        P(None, "mp"),
        P(),
        P(None, "mp"),
        P(None, "mp"),
        P("mp", None),
        P(("dp", "mp"), None),
        P(),
        P(),
        P(),
    )
    out_specs = (
        P(("dp", "mp"), None),
        P(("dp", "mp"), None),
        P(),
        P("dp", "mp"),
        P("dp", "mp"),
        P("dp", "mp"),
        P("mp", "dp"),
        P(None, "mp"),
        P(),
        P("dp", "mp"),
        P("dp", "mp"),
        P("mp", "dp"),
    )
    return jax.shard_map(
        functools.partial(shards, mesh),
        mesh=mesh,
        in_specs=in_specs,
        out_specs=out_specs,
        check_vma=False,
    )
```

time: 1240 us -> 191 us (0.15)
  blocking collectives: 767 us -> 0 us
  local copies, waits for them, and re-layouts: 292 us -> 37.9 us
  Pallas kernels: 0 us -> 150 us
  waiting for transfers between devices: 101 us -> 0 us
  matrix products: 43.2 us -> 1.45 us
  between operations: 15.7 us -> 0.73 us
    unnamed x1 -> x0, blocking collectives: 675 us -> none
    gather x2 -> x0, local copies, waits for them, and re-layouts: 236 us -> none  [block_scores(): bias_rows = jnp.take(bias_by_offset, offsets, axis=1)]
    pallas_call x0 -> x1, Pallas kernels: none -> 150 us  [shards(): pl.pallas_call(functools.partial(layer_kernel, cfg), out_shape=[jax.Shape...]
    unnamed x13 -> x0, waiting for transfers between devices: 101 us -> none
    psum x2 -> x0, blocking collectives: 81.8 us -> none  [the longest x1 43.8 us: shards(): bias_total = lax.psum(bias_grad, 'dp')]
    dot_general x23 -> x1, matrix products: 43.2 us -> 1.45 us  [shards(): lax.dot_general(onehot, diagonals, (((1,), (1,)), ((), ())), precision=la...]
    unnamed x108 -> x22, local copies, waits for them, and re-layouts: 48.7 us -> 27.7 us
  transfers between devices with their start and end apart: 8 -> 0, of which waited for: 3 -> 0; matrix products, arithmetic and copies ran while one was open for 60% -> 0% of each run, Pallas kernels for 0% -> 0%
where the time goes in v1:
time: 191 us; the launch traced here: 190 us
  Pallas kernels  150 us (79%)
  local copies, waits for them, and re-layouts  37.9 us (20%)
    pallas_call x1, Pallas kernels, shards(): pl.pallas_call(functools.partial(layer_kernel, cfg), out_shape=[jax.Shape...  150 us
    unnamed x22, local copies, waits for them, and re-layouts  27.7 us

profile of v1, /device:TPU:0, one launch (start us, length us, event | category | flops | bytes accessed | tf_op | source)
XLA Modules:
  0.0 190.1 jit_solution(15866618274068922328)
XLA Ops:
  0.6 1.3 pad.4
  1.9 1.3 reshape.46.gain_one
  3.2 1.3 reshape.47.gain_two
  4.5 1.4 copy.43.position_bias
  5.9 1.9 %copy.39.hidden_hbm = bf16[128,1472]{1,0:T(8,128)(2,1)} copy(bf16[128,1472]{0,1:T(8,128)(2,1)} %param.15) | data formatting | bytes 753664 | tf_op args[0]
  7.8 1.9 %copy.45.cot_hbm = bf16[128,1472]{1,0:T(8,128)(2,1)} copy(bf16[128,1472]{0,1:T(8,128)(2,1)} %param.26) | data formatting | bytes 753664 | tf_op args[11]
  9.7 2.2 %copy.40.wq_hbm = bf16[1472,192]{1,0:T(8,128)(2,1)} copy(bf16[1472,192]{0,1:T(8,128)(2,1)} %param.17) | data formatting | bytes 1130496 | tf_op args[2]
  11.9 2.2 %copy.41.wk_hbm = bf16[1472,192]{1,0:T(8,128)(2,1)} copy(bf16[1472,192]{0,1:T(8,128)(2,1)} %param.18) | data formatting | bytes 1130496 | tf_op args[3]
  14.1 2.2 %copy.42.wv_hbm = bf16[1472,192]{1,0:T(8,128)(2,1)} copy(bf16[1472,192]{0,1:T(8,128)(2,1)} %param.19) | data formatting | bytes 1130496 | tf_op args[4]
  16.3 8.3 %copy.44.wd_hbm = bf16[1792,1472]{1,0:T(8,128)(2,1)} copy(bf16[1792,1472]{0,1:T(8,128)(2,1)} %param.25) | data formatting | bytes 10551296 | tf_op args[10]
  24.6 0.0 copy-start.1
  24.6 150.1 %shard_map.238 = (f32[128,1472]{1,0:T(8,128)}, f32[128,1472]{1,0:T(8,128)}, f32[8,1536]{1,0:T(8,128)}, f32[24,96,256]{2,1,0:T(8,128)}) custom-call(bf16[128,1472]{1,0:T(8,128)(2,1)} %copy.39.hidden_hbm, f32[1,1472]{1,0:T(1,128)} %reshape.46.gain_one, bf16[1472,192]{1,0:T(8,128)(2,1)} %copy.40.wq_hbm, bf16[1472,192]{1,0:T(8,128)(2,1)} %copy.41.wk_hbm, ...), custom_call_target="tpu_custom_call" | custom-call | flops 14000000000 | bytes 24000000 | tf_op jit(solution)/shard_map/pallas_call | solution.py:678
  174.7 2.3 %copy.50 = f32[128,1472]{0,1:T(8,128)} copy(f32[128,1472]{1,0:T(8,128)} %get-tuple-element.32) | data formatting | bytes 1507328
  176.9 0.0 copy-done.1
  176.9 1.4 fusion
  178.4 1.5 slice_reduce_fusion
  179.9 1.0 slice_bitcast_fusion.3
  180.9 1.7 slice_bitcast_fusion
  182.6 0.4 copy.58
  183.0 0.1 pad.8
  183.0 1.1 copy.56
  184.1 0.2 copy.46
  184.3 0.1 pad.5
  184.4 0.0 copy-start
  184.4 0.1 copy.53
  184.4 0.8 slice_bitcast_fusion.4
  185.2 0.7 copy.52
  186.0 0.4 copy.48
  186.4 0.1 pad.7
  186.4 1.1 copy.55
  187.5 0.4 copy.47
  187.9 0.1 pad.6
  187.9 1.1 copy.54
  189.0 0.0 copy-done
  189.0 1.1 copy.51
Async XLA Ops:
  24.6 152.4 %copy-start.1 = (s32[511]{0:T(512)S(1)}, s32[511]{0:T(512)}, u32[]{:S(2)}) copy-start(s32[511]{0:T(512)} %param.29) | copy-start | bytes 6136
  184.4 4.6 %copy-start = (f32[128,1472]{1,0:T(8,128)S(1)}, f32[128,1472]{1,0:T(8,128)}, u32[]{:S(2)}) copy-start(f32[128,1472]{1,0:T(8,128)} %get-tuple-element.33) | copy-start | bytes 2260996

commit v2 on v1

v2 whole, which is shorter than its diff:
```python
import functools
import math

import jax
import jax.numpy as jnp
from jax import lax
from jax.experimental import pallas as pl
from jax.experimental.pallas import tpu as pltpu
from jax.sharding import PartitionSpec as P

DKV = 64
CW = 256
EPS = 1e-06
LAG = 3
GAP = 2
SLOTS = 3
STEP = 64
MROWS = 368
BF = jnp.bfloat16
F32 = jnp.float32
MESH = pl.DeviceIdType.MESH
GELU_C = math.sqrt(2.0 / math.pi)


def dot(left, right):
    return lax.dot_general(left, right, (((1,), (0,)), ((), ())), preferred_element_type=F32)


def dot_nt(left, right):
    return lax.dot_general(left, right, (((1,), (1,)), ((), ())), preferred_element_type=F32)


def dot_tn(left, right):
    return lax.dot_general(left, right, (((0,), (0,)), ((), ())), preferred_element_type=F32)


def blocks_of(extent, step):
    return [slice(begin, min(begin + step, extent)) for begin in range(0, extent, step)]


def fold(block):
    return jnp.sum(block.reshape(block.shape[0] // 8, 8, block.shape[1]), axis=0)


class Sizes:
    def __init__(self, dp, local_rows, width, head_width, hidden, buckets):
        self.dp = dp
        self.bits = dp.bit_length() - 1
        self.local_rows = local_rows
        self.seq = 2 * local_rows
        self.width = width
        self.head_width = head_width
        self.heads = head_width // DKV
        self.hidden = hidden
        self.buckets = buckets
        self.shard = width // dp
        self.shard_pad = -(-self.shard // 16) * 16
        self.quarter = self.shard_pad * dp // 4
        self.ff_chunks = hidden // CW
        self.ff_total = 3 * self.ff_chunks
        self.chunks = self.ff_total + 4 * head_width // CW
        self.stage_rows = [self.quarter >> k for k in range(self.bits - 1)]
        self.stages = len(self.stage_rows)
        self.wide = -(-width // 256) * 256
        self.tall = width + self.shard_pad


def layer_kernel(
    cfg,
    hidden_hbm,
    gain_one,
    wq_hbm,
    wk_hbm,
    wv_hbm,
    wo_hbm,
    position_bias,
    gain_two,
    wg_hbm,
    wu_hbm,
    wd_hbm,
    cot_hbm,
    lengths,
    groups,
    bucket_ids,
    layer_out,
    input_grad,
    small_out,
    ff_out,
    query_out,
    key_out,
    value_out,
    output_out,
    hid,
    cot_raw,
    cot,
    gains,
    wqkv,
    wo,
    wo_t,
    wg,
    wu,
    wd,
    normed_one,
    normed_two,
    middle,
    qkv,
    probs,
    attended,
    trans,
    left_own,
    left_in,
    right_own,
    right_in,
    out_acc,
    grad_acc,
    grad_send,
    grad_in,
    part_send,
    part_in,
    back_send,
    back_in,
    grad_branch,
    grad_qkv,
    small,
    small_in,
    att_final,
    *rest,
):
    stages = cfg.stages
    stage_own = rest[:stages]
    stage_send = rest[stages : 2 * stages]
    stage_in = rest[2 * stages : 3 * stages]
    (
        load_sem,
        weight_sem,
        pair_send_sem,
        pair_recv_sem,
        left_send_sem,
        left_recv_sem,
        right_send_sem,
        right_recv_sem,
        stage_send_sem,
        stage_recv_sem,
        small_send_sem,
        small_recv_sem,
    ) = rest[3 * stages :]

    seq, rows, width, hw, heads = cfg.seq, cfg.local_rows, cfg.width, cfg.head_width, cfg.heads
    me = lax.axis_index("dp")
    core = lax.axis_index("mp")
    bit = [lax.rem(lax.div(me, 1 << k), 2) for k in range(cfg.bits)]
    peer = [me + (1 - 2 * bit[k]) * (1 << k) for k in range(cfg.bits)]
    sibling = (me, 1 - core)
    own_lanes = pl.ds(pl.multiple_of(core * rows, rows), rows)
    other_lanes = pl.ds(pl.multiple_of((1 - core) * rows, rows), rows)

    def send(src, dst, send_sem, recv_sem, target):
        return pltpu.make_async_remote_copy(
            src_ref=src,
            dst_ref=dst,
            send_sem=send_sem,
            recv_sem=recv_sem,
            device_id=target,
            device_id_type=MESH,
        )

    loads = [
        pltpu.make_async_copy(hidden_hbm, hid.at[core], load_sem.at[0]),
        pltpu.make_async_copy(cot_hbm, cot_raw.at[core], load_sem.at[1]),
        pltpu.make_async_copy(wq_hbm, wqkv.at[0], load_sem.at[2]),
        pltpu.make_async_copy(wk_hbm, wqkv.at[1], load_sem.at[3]),
        pltpu.make_async_copy(wv_hbm, wqkv.at[2], load_sem.at[4]),
        pltpu.make_async_copy(wo_hbm, wo.at[core], load_sem.at[5]),
    ]
    for load in loads:
        load.start()

    def weight_loads(chunk, slot):
        columns = pl.ds(pl.multiple_of(chunk * CW, CW), CW)
        return [
            pltpu.make_async_copy(src.at[:, columns], dst.at[slot], weight_sem.at[slot, index])
            for index, (src, dst) in enumerate(((wg_hbm, wg), (wu_hbm, wu), (wd_hbm, wd)))
        ]

    barrier = pltpu.get_barrier_semaphore()
    pl.semaphore_signal(barrier, inc=1, device_id=sibling, device_id_type=MESH)
    for k in range(cfg.bits):
        pl.semaphore_signal(barrier, inc=1, device_id=(peer[k], core), device_id_type=MESH)
    for index, gain in enumerate((gain_one, gain_two)):
        for block in blocks_of(width, 128):
            size = block.stop - block.start
            gains[index, block, :] = jnp.transpose(
                jnp.broadcast_to(gain[0:1, block], (128, size))
            )
    pl.semaphore_wait(barrier, cfg.bits + 1)

    pair_hid = send(
        hidden_hbm, hid.at[core], pair_send_sem.at[0], pair_recv_sem.at[0], sibling
    )
    pair_cot = send(
        cot_hbm, cot_raw.at[core], pair_send_sem.at[1], pair_recv_sem.at[1], sibling
    )
    pair_wo = send(wo_hbm, wo.at[core], pair_send_sem.at[2], pair_recv_sem.at[2], sibling)
    pair_hid.start()
    pair_cot.start()
    pair_wo.start()
    pair_att = send(
        attended.at[core], attended.at[core], pair_send_sem.at[3], pair_recv_sem.at[3], sibling
    )
    pair_grad = send(grad_send, grad_in, pair_send_sem.at[4], pair_recv_sem.at[4], sibling)
    pair_part = send(part_send, part_in, pair_send_sem.at[5], pair_recv_sem.at[5], sibling)
    pair_back = send(back_send, back_in, pair_send_sem.at[6], pair_recv_sem.at[6], sibling)

    for slot in range(2):
        for load in weight_loads(slot, slot):
            load.start()

    group_len = jnp.int32(0)
    for item in range(lengths.shape[0]):
        group_len = group_len + jnp.where(groups[item] == me, lengths[item], 0)

    left_axis = (0, 1, 1, 1)

    def build_left(source, which):
        first = left_axis[which]
        for index in range(cfg.dp):
            low = (index & 1, (index >> 1) & 1)
            place = 0
            for k in range(2, cfg.bits):
                place = 2 * place + ((index >> k) & 1)
            block = source[index * cfg.shard : index * cfg.shard + cfg.shard_pad, :]
            left_own[
                which,
                low[first],
                low[1 - first],
                place * cfg.shard_pad : (place + 1) * cfg.shard_pad,
                :,
            ] = block.astype(BF)

    def left_copy(which):
        first = left_axis[which]
        return send(
            left_own.at[which, 1 - bit[first]],
            left_in.at[which],
            left_send_sem.at[which],
            left_recv_sem.at[which],
            (peer[first], core),
        )

    def right_copy(chunk, first):
        return send(
            right_own.at[chunk],
            right_in.at[chunk],
            right_send_sem.at[chunk],
            right_recv_sem.at[chunk],
            (peer[first], core),
        )

    for scratch in (trans, grad_acc):
        scratch[width:, :] = jnp.zeros((cfg.tall - width, seq), F32)

    step_rows = STEP
    steps = width // step_rows

    def rows_at(step):
        return pl.ds(pl.multiple_of(step * step_rows, step_rows), step_rows)

    def whole(ref, block):
        return jnp.concatenate([ref[0, block, :], ref[1, block, :]], axis=1)

    def gain_at(index, block, lanes):
        part = gains[index, block, :]
        return jnp.concatenate([part] * (lanes // 128), axis=1)

    def column_sum(term, lanes):
        zero = jnp.zeros((8, lanes), F32)
        total = lax.fori_loop(0, steps, lambda i, acc: acc + fold(term(rows_at(i))), zero)
        return jnp.sum(total, axis=0, keepdims=True)

    def inverse_rms(term, lanes):
        def square(block):
            x = term(block)
            return x * x

        return lax.rsqrt(column_sum(square, lanes) * (1.0 / width) + EPS)

    loads[0].wait()
    pair_hid.wait()

    def x_at(block):
        return whole(hid, block).astype(F32)

    inv_one = inverse_rms(x_at, seq)

    def norm_one_rows(step, carry):
        block = rows_at(step)
        normed = x_at(block) * inv_one * gain_at(0, block, seq)
        trans[block, :] = normed
        normed_one[block, :] = normed.astype(BF)
        return carry

    lax.fori_loop(0, steps, norm_one_rows, 0)

    for part in range(3):
        loads[2 + part].wait()
        qkv[part] = dot(wqkv[part], normed_one[...]).astype(BF)

    key_valid = lax.broadcasted_iota(jnp.int32, (seq, seq), 0) < group_len
    ids = bucket_ids[...]
    for head in range(heads):
        part = slice(head * DKV, (head + 1) * DKV)
        by_offset = jnp.zeros(ids.shape, F32)
        for bucket in range(cfg.buckets):
            by_offset = jnp.where(ids == bucket, position_bias[head, bucket], by_offset)
        bias = pltpu.roll(
            jnp.broadcast_to(by_offset, (seq, 2 * seq)),
            seq + 1,
            1,
            stride=1,
            stride_axis=0,
        )[:, :seq]
        scores = dot_tn(qkv[1, part, :], qkv[0, part, :]) + bias
        scores = jnp.where(key_valid, scores, -1e30)
        exps = jnp.exp(scores - jnp.max(scores, axis=0, keepdims=True))
        prob = exps / jnp.sum(exps, axis=0, keepdims=True)
        probs[head] = prob
        attended[core, part, :] = dot(qkv[2, part, :], prob.astype(BF)).astype(BF)
    pair_att.start()

    build_left(trans, 2)
    left_copy(2).start()
    loads[1].wait()
    pair_cot.wait()
    row_valid = lax.broadcasted_iota(jnp.int32, (step_rows, seq), 1) < group_len

    def mask_rows(step, carry):
        block = rows_at(step)
        trans[block, :] = jnp.where(row_valid, whole(cot_raw, block).astype(F32), 0.0)
        return carry

    lax.fori_loop(0, steps, mask_rows, 0)
    build_left(trans, 0)
    left_copy(0).start()
    for block in blocks_of(width, 128):
        cot[:, block] = jnp.transpose(trans[block, :]).astype(BF)

    loads[5].wait()
    pair_wo.wait()
    for block in blocks_of(width, 128):
        wo_t[block, :] = jnp.transpose(
            jnp.concatenate([wo[0, :, block], wo[1, :, block]], axis=0).astype(F32)
        ).astype(BF)
    pair_att.wait()
    both = attended[...].reshape(2 * hw, seq)
    for block in blocks_of(width, MROWS):
        middle[block, :] = x_at(block) + dot(wo_t[block, :], both)

    inv_two = inverse_rms(lambda block: middle[block, :], seq)

    def norm_two_rows(step, carry):
        block = rows_at(step)
        trans[block, :] = middle[block, :] * inv_two * gain_at(1, block, seq)
        out_acc[block, :] = jnp.zeros((step_rows, seq), F32)
        grad_acc[block, :] = jnp.zeros((step_rows, seq), F32)
        return carry

    lax.fori_loop(0, steps, norm_two_rows, 0)
    build_left(trans, 1)
    left_copy(1).start()
    for block in blocks_of(width, 128):
        normed_two[:, block] = jnp.transpose(trans[block, :]).astype(BF)
    small[...] = jnp.zeros_like(small)

    def feed_forward(chunk):
        slot = lax.rem(chunk, 2)
        for load in weight_loads(chunk, slot):
            load.wait()
        normed = normed_two[...]
        gate = dot(normed, wg[slot])
        up = dot(normed, wu[slot])
        grad_hidden = dot(cot[...], wd[slot])
        square = gate * gate
        tanh = jnp.tanh(GELU_C * (gate + 0.044715 * (square * gate)))
        half = 0.5 * (1.0 + tanh)
        gelu = gate * half
        slope = half + (0.5 * GELU_C) * gate * (1.0 - tanh * tanh) * (
            1.0 + (3 * 0.044715) * square
        )
        hidden = (gelu * up).astype(BF)
        grad_gate = (grad_hidden * up * slope).astype(BF)
        grad_up = (grad_hidden * gelu).astype(BF)
        base = 3 * chunk
        right_own[base] = hidden
        right_own[base + 1] = grad_gate
        right_own[base + 2] = grad_up
        right_copy(base, 0).start()
        right_copy(base + 1, 1).start()
        right_copy(base + 2, 1).start()
        for block in blocks_of(width, MROWS):
            out_acc[block, :] += dot_nt(wd[slot, block, :], hidden)
            grad_acc[block, :] += dot_nt(wg[slot, block, :], grad_gate) + dot_nt(
                wu[slot, block, :], grad_up
            )

        @pl.when(chunk < cfg.ff_chunks - 2)
        def _():
            for load in weight_loads(chunk + 2, slot):
                load.start()

    def exchange_sums():
        grad_send[...] = grad_acc[:width, :].astype(BF)
        pair_grad.start()
        part_send[...] = out_acc[:, other_lanes].astype(BF)
        pair_part.start()

    def lane_mask(shape, dimension):
        lane = lax.broadcasted_iota(jnp.int32, shape, dimension)
        return (lax.div(lane, rows) == core).astype(F32)

    def lane_sums(weights, source):
        return lax.dot_general(
            weights,
            source,
            (((1,), (1,)), ((), ())),
            precision=lax.Precision.HIGHEST,
            preferred_element_type=F32,
        )[0:1, :]

    def norm_two_back():
        pair_grad.wait()

        def grad_at(block):
            return grad_acc[block, :] + grad_in[block, :].astype(F32)

        inv = inverse_rms(lambda block: middle[block, :], seq)
        inner = (
            column_sum(
                lambda block: grad_at(block) * gain_at(1, block, seq) * middle[block, :], seq
            )
            * inv
            * (1.0 / width)
        )

        def back_rows(step, carry):
            block = rows_at(step)
            grad = grad_at(block)
            unit = middle[block, :] * inv
            masked = jnp.where(row_valid, whole(cot_raw, block).astype(F32), 0.0)
            total = masked + inv * (grad * gain_at(1, block, seq) - unit * inner)
            trans[block, :] = grad * unit
            grad_acc[block, :] = total
            grad_branch[block, :] = total.astype(BF)
            return carry

        lax.fori_loop(0, steps, back_rows, 0)
        build_left(grad_acc, 3)
        left_copy(3).start()
        mask = lane_mask((8, seq), 1)
        small[1:2, :width] = lane_sums(mask, trans[:width, :])

    def attention_back():
        grad_att = dot(wo[core], grad_branch[...]).astype(BF)
        flip = (
            lax.broadcasted_iota(jnp.int32, (seq, seq), 0)
            + lax.broadcasted_iota(jnp.int32, (seq, seq), 1)
            == seq - 1
        ).astype(BF)
        for head in range(heads):
            part = slice(head * DKV, (head + 1) * DKV)
            grad_mixed = grad_att[part, :]
            prob = probs[head]
            grad_probs = dot_tn(qkv[2, part, :], grad_mixed)
            inner = jnp.sum(prob * grad_probs, axis=0, keepdims=True)
            grad_scores = (prob * (grad_probs - inner)).astype(BF)
            grad_qkv[0, part, :] = dot(qkv[1, part, :], grad_scores).astype(BF)
            grad_qkv[1, part, :] = dot_nt(qkv[0, part, :], grad_scores).astype(BF)
            grad_qkv[2, part, :] = dot_nt(grad_mixed, prob.astype(BF)).astype(BF)
            flipped = jnp.concatenate(
                [dot(flip, grad_scores), jnp.zeros((seq, seq), F32)], axis=1
            )
            skewed = pltpu.roll(flipped, 0, 1, stride=1, stride_axis=0)
            small[2 + head : 3 + head, : 2 * seq] = jnp.sum(skewed, axis=0, keepdims=True)
        joined = jnp.concatenate(
            [grad_qkv[...].reshape(3 * hw, seq), attended[core]], axis=0
        ).astype(F32)
        for index in range(cfg.chunks - cfg.ff_total):
            chunk = cfg.ff_total + index
            right_own[chunk] = jnp.transpose(joined[index * CW : (index + 1) * CW, :]).astype(BF)
            right_copy(chunk, 1).start()

    def norm_one_sums():
        for block in blocks_of(width, 128):
            back_send[block, :] = sum(
                dot_tn(wqkv[part, :, block], grad_qkv[part, :, other_lanes]) for part in range(3)
            ).astype(BF)
        pair_back.start()
        for block in blocks_of(width, 128):
            input_grad[block, :] = sum(
                dot_tn(wqkv[part, :, block], grad_qkv[part, :, own_lanes]) for part in range(3)
            )

    def small_copy(k):
        target = sibling if k == cfg.bits else (peer[k], core)
        return send(
            small, small_in.at[k], small_send_sem.at[k], small_recv_sem.at[k], target
        )

    def finish_rows():
        pair_part.wait()
        pair_back.wait()

        def x_own(block):
            return hid[core, block, :].astype(F32)

        def grad_at(block):
            return input_grad[block, :] + back_in[block, :].astype(F32)

        inv = inverse_rms(x_own, rows)
        inner = (
            column_sum(lambda block: grad_at(block) * gain_at(0, block, rows) * x_own(block), rows)
            * inv
            * (1.0 / width)
        )

        def last_rows(step, carry):
            block = rows_at(step)
            grad = grad_at(block)
            unit = x_own(block) * inv
            input_grad[block, :] = grad_acc[block, own_lanes] + inv * (
                grad * gain_at(0, block, rows) - unit * inner
            )
            layer_out[block, :] = (
                middle[block, own_lanes]
                + out_acc[block, own_lanes]
                + part_in[block, :].astype(F32)
            )
            trans[block, :rows] = grad * unit
            return carry

        lax.fori_loop(0, steps, last_rows, 0)
        small[0:1, :width] = lane_sums(jnp.ones((8, rows), F32), trans[:width, :rows])
        small_copy(0).start()

    def small_stage(k):
        small_copy(k).wait()
        if k == cfg.bits:
            row = lax.broadcasted_iota(jnp.int32, small.shape, 0)
            small_out[...] = small[...] + jnp.where(row < 2, small_in[k], 0.0)
        else:
            small[...] = small[...] + small_in[k]
            small_copy(k + 1).start()

    def chunk_kind(chunk):
        tail_part = lax.div(chunk, cfg.ff_total)
        kind = lax.rem(chunk, 3)
        which = (1 - tail_part) * lax.div(kind + 1, 2) + 2 * tail_part
        y_first = 1 - lax.div(2 - which, 2)
        return which, y_first

    def stage_copy(k, chunk, target):
        slot = lax.rem(chunk, SLOTS)
        return send(
            stage_send[k].at[slot],
            stage_in[k].at[chunk],
            stage_send_sem.at[k, slot],
            stage_recv_sem.at[k, chunk],
            (target, core),
        )

    def stage_target(k, chunk):
        if k > 0:
            return peer[k + 1]
        y_first = chunk_kind(chunk)[1]
        return y_first * peer[0] + (1 - y_first) * peer[1]

    def form(chunk):
        which, y_first = chunk_kind(chunk)
        slot = lax.rem(chunk, SLOTS)
        first_bit = y_first * bit[1] + (1 - y_first) * bit[0]
        second_bit = y_first * bit[0] + (1 - y_first) * bit[1]

        @pl.when(chunk == 0)
        def _():
            left_copy(0).wait()

        @pl.when(chunk == 1)
        def _():
            left_copy(1).wait()

        @pl.when(chunk == cfg.ff_total)
        def _():
            left_copy(2).wait()

        right_copy(chunk, 0).wait()

        def product(left, quarter):
            return dot(left_own[left, first_bit, quarter], right_own[chunk]) + dot(
                left_in[left, quarter], right_in[chunk]
            )

        @pl.when(chunk < cfg.chunks - 1)
        def _():
            stage_send[0][slot] = product(which, 1 - second_bit).astype(BF)
            stage_copy(0, chunk, stage_target(0, chunk)).start()
            stage_own[0][slot] = product(which, second_bit)

        @pl.when(chunk == cfg.chunks - 1)
        def _():
            left_copy(3).wait()
            split = lax.broadcasted_iota(jnp.int32, (cfg.quarter, CW), 1) < CW - hw

            def mixed(quarter):
                return jnp.where(split, product(2, quarter), product(3, quarter))

            stage_send[0][slot] = mixed(1 - second_bit).astype(BF)
            stage_copy(0, chunk, stage_target(0, chunk)).start()
            stage_own[0][slot] = mixed(second_bit)

    def halve(k, chunk):
        slot = lax.rem(chunk, SLOTS)
        stage_copy(k - 1, chunk, stage_target(k - 1, chunk)).wait()
        if k == stages:
            result = stage_own[k - 1][slot] + stage_in[k - 1][chunk].astype(F32)

            @pl.when(chunk < cfg.ff_total)
            def _():
                columns = pl.ds(pl.multiple_of(lax.div(chunk, 3) * CW, CW), CW)
                ff_out[lax.rem(chunk, 3), :, columns] = result[: cfg.shard, :]

            @pl.when(chunk >= cfg.ff_total)
            def _():
                att_final[lax.rem(chunk, cfg.ff_total)] = result

            return
        half = cfg.stage_rows[k]
        mine = bit[k + 1]

        def total(which):
            part = pl.ds(pl.multiple_of(which * half, 16), half)
            return stage_own[k - 1][slot, part, :] + stage_in[k - 1][chunk, part, :].astype(F32)

        stage_send[k][slot] = total(1 - mine).astype(BF)
        stage_copy(k, chunk, stage_target(k, chunk)).start()
        stage_own[k][slot] = total(mine)

    last_ff = 3 * (cfg.ff_chunks - 1)
    pieces = [exchange_sums, norm_two_back, attention_back, norm_one_sums, finish_rows]
    pieces += [functools.partial(small_stage, k) for k in range(cfg.bits + 1)]
    ticks = max(LAG + cfg.chunks + GAP * stages, last_ff + len(pieces))

    def tick(t, carry):
        for k in range(stages, 0, -1):
            chunk = t - LAG - GAP * k

            @pl.when(jnp.logical_and(chunk >= 0, chunk < cfg.chunks))
            def _(k=k, chunk=chunk):
                halve(k, chunk)

        new = t - LAG

        @pl.when(jnp.logical_and(new >= 0, new < cfg.chunks))
        def _():
            form(new)

        @pl.when(jnp.logical_and(lax.rem(t, 3) == 0, t <= last_ff))
        def _():
            feed_forward(lax.div(t, 3))

        for index, piece in enumerate(pieces):

            @pl.when(t == last_ff + index)
            def _(piece=piece):
                piece()

        return carry

    lax.fori_loop(0, ticks, tick, 0)

    flat = jnp.concatenate([att_final[index] for index in range(cfg.chunks - cfg.ff_total)], axis=1)
    for part, ref in enumerate((query_out, key_out, value_out)):
        ref[...] = flat[: cfg.shard, part * hw : (part + 1) * hw]
    output_out[...] = jnp.transpose(flat[:, 3 * hw :])[:, : cfg.shard]


def shards(
    mesh,
    hidden_in,
    attention_gain,
    query_weight,
    key_weight,
    value_weight,
    output_weight,
    position_bias,
    feedforward_gain,
    gate_weight,
    up_weight,
    down_weight,
    cotangent,
    item_lengths,
    item_group,
    bucket_ids,
):
    rows, width = hidden_in.shape
    hw = query_weight.shape[1]
    hidden = gate_weight.shape[1]
    buckets = position_bias.shape[0]
    cfg = Sizes(mesh.shape["dp"], rows, width, hw, hidden, buckets)
    seq, stages, shard = cfg.seq, cfg.stages, cfg.shard
    any_spec = pl.BlockSpec(memory_space=pl.ANY)
    vmem = pl.BlockSpec(memory_space=pltpu.VMEM)
    smem = pl.BlockSpec(memory_space=pltpu.SMEM)
    small_shape = (8, cfg.wide)
    scratch = [
        pltpu.VMEM((2, width, rows), BF),
        pltpu.VMEM((2, width, rows), BF),
        pltpu.VMEM((seq, width), BF),
        pltpu.VMEM((2, width, 128), F32),
        pltpu.VMEM((3, hw, width), BF),
        pltpu.VMEM((2, hw, width), BF),
        pltpu.VMEM((width, 2 * hw), BF),
        pltpu.VMEM((2, width, CW), BF),
        pltpu.VMEM((2, width, CW), BF),
        pltpu.VMEM((2, width, CW), BF),
        pltpu.VMEM((width, seq), BF),
        pltpu.VMEM((seq, width), BF),
        pltpu.VMEM((width, seq), F32),
        pltpu.VMEM((3, hw, seq), BF),
        pltpu.VMEM((cfg.heads, seq, seq), F32),
        pltpu.VMEM((2, hw, seq), BF),
        pltpu.VMEM((cfg.tall, seq), F32),
        pltpu.VMEM((4, 2, 2, cfg.quarter, seq), BF),
        pltpu.VMEM((4, 2, cfg.quarter, seq), BF),
        pltpu.VMEM((cfg.chunks, seq, CW), BF),
        pltpu.VMEM((cfg.chunks, seq, CW), BF),
        pltpu.VMEM((width, seq), F32),
        pltpu.VMEM((cfg.tall, seq), F32),
        pltpu.VMEM((width, seq), BF),
        pltpu.VMEM((width, seq), BF),
        pltpu.VMEM((width, rows), BF),
        pltpu.VMEM((width, rows), BF),
        pltpu.VMEM((width, rows), BF),
        pltpu.VMEM((width, rows), BF),
        pltpu.VMEM((width, seq), BF),
        pltpu.VMEM((3, hw, seq), BF),
        pltpu.VMEM(small_shape, F32),
        pltpu.VMEM((cfg.bits + 1,) + small_shape, F32),
        pltpu.VMEM((cfg.chunks - cfg.ff_total, cfg.shard_pad, CW), F32),
    ]
    scratch += [pltpu.VMEM((SLOTS, size, CW), F32) for size in cfg.stage_rows]
    scratch += [pltpu.VMEM((SLOTS, size, CW), BF) for size in cfg.stage_rows]
    scratch += [pltpu.VMEM((cfg.chunks, size, CW), BF) for size in cfg.stage_rows]
    dma = pltpu.SemaphoreType.DMA
    scratch += [
        dma((6,)),
        dma((2, 3)),
        dma((7,)),
        dma((7,)),
        dma((4,)),
        dma((4,)),
        dma((cfg.chunks,)),
        dma((cfg.chunks,)),
        dma((stages, SLOTS)),
        dma((stages, cfg.chunks)),
        dma((cfg.bits + 1,)),
        dma((cfg.bits + 1,)),
    ]
    reversed_ids = jnp.pad(
        jnp.flip(bucket_ids), (0, 2 * seq - bucket_ids.shape[0]), constant_values=-1
    )
    (
        layer_out,
        input_grad,
        small_sum,
        ff_sum,
        query_sum,
        key_sum,
        value_sum,
        output_sum,
    ) = pl.pallas_call(
        functools.partial(layer_kernel, cfg),
        out_shape=[
            jax.ShapeDtypeStruct((width, rows), F32),
            jax.ShapeDtypeStruct((width, rows), F32),
            jax.ShapeDtypeStruct(small_shape, F32),
            jax.ShapeDtypeStruct((3, shard, hidden), F32),
            jax.ShapeDtypeStruct((shard, hw), F32),
            jax.ShapeDtypeStruct((shard, hw), F32),
            jax.ShapeDtypeStruct((shard, hw), F32),
            jax.ShapeDtypeStruct((hw, shard), F32),
        ],
        in_specs=[
            any_spec,
            vmem,
            any_spec,
            any_spec,
            any_spec,
            any_spec,
            smem,
            vmem,
            any_spec,
            any_spec,
            any_spec,
            any_spec,
            smem,
            smem,
            vmem,
        ],
        out_specs=[vmem] * 8,
        scratch_shapes=scratch,
        compiler_params=pltpu.CompilerParams(
            collective_id=0, has_side_effects=True, vmem_limit_bytes=60 * 1024 * 1024
        ),
        cost_estimate=pl.CostEstimate(
            flops=14 * 10**9, bytes_accessed=24 * 10**6, transcendentals=10**6
        ),
    )(
        hidden_in.T,
        attention_gain.reshape(1, width),
        query_weight.T,
        key_weight.T,
        value_weight.T,
        output_weight,
        position_bias.T,
        feedforward_gain.reshape(1, width),
        gate_weight,
        up_weight,
        down_weight.T,
        cotangent.T,
        item_lengths,
        item_group,
        reversed_ids.reshape(1, -1),
    )
    onehot = (
        jnp.flip(bucket_ids)[None, :] == jnp.arange(buckets, dtype=jnp.int32)[:, None]
    ).astype(F32)
    diagonals = small_sum[2 : 2 + cfg.heads, : bucket_ids.shape[0]]
    bias_total = lax.dot_general(
        onehot, diagonals, (((1,), (1,)), ((), ())), precision=lax.Precision.HIGHEST
    )
    return (
        layer_out.T,
        input_grad.T,
        small_sum[0, :width],
        query_sum,
        key_sum,
        value_sum,
        output_sum,
        bias_total,
        small_sum[1, :width],
        ff_sum[1],
        ff_sum[2],
        ff_sum[0].T,
    )


def solution(mesh):
    in_specs = (
        P(("dp", "mp"), None),
        P(),
        P(None, "mp"),
        P(None, "mp"),
        P(None, "mp"),
        P("mp", None),
        P(None, "mp"),
        P(),
        P(None, "mp"),
        P(None, "mp"),
        P("mp", None),
        P(("dp", "mp"), None),
        P(),
        P(),
        P(),
    )
    out_specs = (
        P(("dp", "mp"), None),
        P(("dp", "mp"), None),
        P(),
        P("dp", "mp"),
        P("dp", "mp"),
        P("dp", "mp"),
        P("mp", "dp"),
        P(None, "mp"),
        P(),
        P("dp", "mp"),
        P("dp", "mp"),
        P("mp", "dp"),
    )
    return jax.shard_map(
        functools.partial(shards, mesh),
        mesh=mesh,
        in_specs=in_specs,
        out_specs=out_specs,
        check_vma=False,
    )
```

time: 191 us -> 164 us (0.86)
  local copies, waits for them, and re-layouts: 37.9 us -> 13.9 us
  Pallas kernels: 150 us -> 147 us
    unnamed x22 -> x18, local copies, waits for them, and re-layouts: 27.7 us -> 6.34 us
    pallas_call x1, Pallas kernels: 150 us -> 147 us  [shards(): pl.pallas_call(functools.partial(layer_kernel, cfg), out_shape=[jax.Shape...]
    transpose x7 -> x1, local copies, waits for them, and re-layouts: 4.8 us -> 2.86 us  [shards(): ff_sum[0]]
where the time goes in v2:
time: 164 us; the launch traced here: 163 us
  Pallas kernels  147 us (90%)
  local copies, waits for them, and re-layouts  13.9 us (8%)
    pallas_call x1, Pallas kernels, shards(): pl.pallas_call(functools.partial(layer_kernel, cfg), out_shape=[jax.Shape...  147 us
    unnamed x18, local copies, waits for them, and re-layouts  6.34 us

profile of v2, /device:TPU:0, one launch (start us, length us, event | category | flops | bytes accessed | tf_op | source)
XLA Modules:
  0.0 163.3 jit_solution(10499424633439329274)
XLA Ops:
  0.6 0.8 reverse
  1.4 0.1 slice.31
  1.5 0.6 pad.4
  2.1 1.3 reshape.34.gain_one
  3.4 1.3 reshape.35.gain_two
  4.7 147.2 %shard_map.238 = (f32[1472,128]{1,0:T(8,128)}, f32[1472,128]{1,0:T(8,128)}, f32[8,1536]{1,0:T(8,128)}, f32[3,92,1792]{2,1,0:T(8,128)}, f32[92,192]{1,0:T(8,128)}...) custom-call(bf16[1472,128]{1,0:T(8,128)(2,1)} %bitcast.27, f32[1,1472]{1,0:T(1,128)} %reshape.34.gain_one, ...), custom_call_target="tpu_custom_call" | custom-call | flops 14000000000 | bytes 24000000 | tf_op jit(solution)/shard_map/pallas_call | solution.py:779
  151.9 0.0 copy-start
  151.9 0.0 copy-start.4
  151.9 0.0 copy-start.3
  151.9 0.0 copy-start.2
  151.9 0.0 copy-start.1
  151.9 1.5 fusion
  153.5 1.5 slice_reduce_fusion
  155.0 2.9 %slice_bitcast_fusion = (f32[1792,92]{0,1:T(8,128)}, f32[92,1792]{1,0:T(8,128)}, f32[92,1792]{1,0:T(8,128)}) fusion(f32[3,92,1792]{2,1,0:T(8,128)} %get-tuple-element.27), kind=kLoop, calls=%fused_computation | loop fusion | bytes 3956736 | tf_op jit(solution)/shard_map/transpose | solution.py:852
  157.8 2.0 %copy.33 = f32[128,1472]{0,1:T(8,128)} copy(f32[128,1472]{0,1:T(8,128)} %bitcast.20) | data formatting | bytes 1507328
  159.9 0.0 copy-done
  159.9 0.9 copy.34
  160.7 0.0 copy-done.4
  160.7 0.6 copy.35
  161.4 0.0 copy-done.3
  161.4 0.6 copy.36
  162.0 0.0 copy-done.2
  162.0 0.6 copy.37
  162.7 0.0 copy-done.1
  162.7 0.6 copy.38
Async XLA Ops:
  151.9 8.0 %copy-start = (f32[1472,128]{1,0:T(8,128)S(1)}, f32[1472,128]{1,0:T(8,128)}, u32[]{:S(2)}) copy-start(f32[1472,128]{1,0:T(8,128)} %get-tuple-element.21) | copy-start | bytes 2260996
  151.9 8.9 %copy-start.4 = (f32[92,192]{1,0:T(8,128)S(1)}, f32[92,192]{1,0:T(8,128)}, u32[]{:S(2)}) copy-start(f32[92,192]{1,0:T(8,128)} %get-tuple-element.48) | copy-start | bytes 211972
  151.9 9.5 %copy-start.3 = (f32[92,192]{1,0:T(8,128)S(1)}, f32[92,192]{1,0:T(8,128)}, u32[]{:S(2)}) copy-start(f32[92,192]{1,0:T(8,128)} %get-tuple-element.49) | copy-start | bytes 211972
  151.9 10.1 %copy-start.2 = (f32[92,192]{1,0:T(8,128)S(1)}, f32[92,192]{1,0:T(8,128)}, u32[]{:S(2)}) copy-start(f32[92,192]{1,0:T(8,128)} %get-tuple-element.50) | copy-start | bytes 211972
  151.9 10.8 %copy-start.1 = (f32[192,92]{1,0:T(8,128)S(1)}, f32[192,92]{1,0:T(8,128)}, u32[]{:S(2)}) copy-start(f32[192,92]{1,0:T(8,128)} %get-tuple-element.51) | copy-start | bytes 211972

commit v3 on v2

--- a/solution.py
+++ b/solution.py
@@ -12,8 +12,11 @@
 CW = 256
 EPS = 1e-06
 LAG = 3
-GAP = 2
-SLOTS = 3
+GAP = 3
+SLOTS = 4
+FF_TICKS = 2
+SMALL_GAP = 3
+AXES = ((0, 1, 2), (1, 0, 2), (2, 1, 0), (2, 1, 0))
 STEP = 64
 MROWS = 368
 BF = jnp.bfloat16
@@ -61,8 +64,9 @@
         self.chunks = self.ff_total + 4 * head_width // CW
         self.stage_rows = [self.quarter >> k for k in range(self.bits - 1)]
         self.stages = len(self.stage_rows)
-        self.wide = -(-width // 256) * 256
+        self.half = -(-width // 256) * 128
         self.tall = width + self.shard_pad
+        self.orders = [axes + tuple(range(3, self.bits)) for axes in AXES]
 
 
 def layer_kernel(
@@ -124,6 +128,7 @@
     small,
     small_in,
     att_final,
+    ids_row,
     *rest,
 ):
     stages = cfg.stages
@@ -137,6 +142,8 @@
         pair_recv_sem,
         left_send_sem,
         left_recv_sem,
+        share_send_sem,
+        share_recv_sem,
         right_send_sem,
         right_recv_sem,
         stage_send_sem,
@@ -187,10 +194,11 @@
     for k in range(cfg.bits):
         pl.semaphore_signal(barrier, inc=1, device_id=(peer[k], core), device_id_type=MESH)
     for index, gain in enumerate((gain_one, gain_two)):
+        line = gain[...].reshape(1, width)
         for block in blocks_of(width, 128):
             size = block.stop - block.start
             gains[index, block, :] = jnp.transpose(
-                jnp.broadcast_to(gain[0:1, block], (128, size))
+                jnp.broadcast_to(line[:, block], (128, size))
             )
     pl.semaphore_wait(barrier, cfg.bits + 1)
 
@@ -219,41 +227,61 @@
     for item in range(lengths.shape[0]):
         group_len = group_len + jnp.where(groups[item] == me, lengths[item], 0)
 
-    left_axis = (0, 1, 1, 1)
-
     def build_left(source, which):
-        first = left_axis[which]
+        order = cfg.orders[which]
         for index in range(cfg.dp):
-            low = (index & 1, (index >> 1) & 1)
+            bits = [(index >> k) & 1 for k in order]
             place = 0
-            for k in range(2, cfg.bits):
-                place = 2 * place + ((index >> k) & 1)
+            for value in bits[2:]:
+                place = 2 * place + value
             block = source[index * cfg.shard : index * cfg.shard + cfg.shard_pad, :]
             left_own[
                 which,
-                low[first],
-                low[1 - first],
+                bits[0],
+                bits[1],
                 place * cfg.shard_pad : (place + 1) * cfg.shard_pad,
                 :,
             ] = block.astype(BF)
 
     def left_copy(which):
-        first = left_axis[which]
+        first = cfg.orders[which][0]
         return send(
-            left_own.at[which, 1 - bit[first]],
-            left_in.at[which],
+            left_own.at[which, 1 - bit[first], core],
+            left_in.at[which, core],
             left_send_sem.at[which],
             left_recv_sem.at[which],
             (peer[first], core),
         )
 
-    def right_copy(chunk, first):
+    def left_share(which):
+        return send(
+            left_in.at[which, core],
+            left_in.at[which, core],
+            share_send_sem.at[which],
+            share_recv_sem.at[which],
+            sibling,
+        )
+
+    def left_pass(which):
+        left_copy(which).wait()
+        left_share(which).start()
+
+    def pick(chunk, level, values):
+        ks = [cfg.orders[which][level] for which in range(3)]
+        if ks[0] == ks[1] == ks[2]:
+            return values[ks[0]]
+        tail_part = lax.div(chunk, cfg.ff_total)
+        hidden_part = (1 - tail_part) * (1 - lax.div(lax.rem(chunk, 3) + 1, 2))
+        parts = (hidden_part, 1 - tail_part - hidden_part, tail_part)
+        return sum(part * values[k] for part, k in zip(parts, ks))
+
+    def right_copy(chunk):
         return send(
             right_own.at[chunk],
             right_in.at[chunk],
             right_send_sem.at[chunk],
             right_recv_sem.at[chunk],
-            (peer[first], core),
+            (pick(chunk, 0, peer), core),
         )
 
     for scratch in (trans, grad_acc):
@@ -306,7 +334,9 @@
         qkv[part] = dot(wqkv[part], normed_one[...]).astype(BF)
 
     key_valid = lax.broadcasted_iota(jnp.int32, (seq, seq), 0) < group_len
-    ids = bucket_ids[...]
+    ids_row[...] = jnp.full(ids_row.shape, -1, jnp.int32)
+    ids_row[:, : bucket_ids.shape[0]] = bucket_ids[...].reshape(1, -1)
+    ids = ids_row[...]
     for head in range(heads):
         part = slice(head * DKV, (head + 1) * DKV)
         by_offset = jnp.zeros(ids.shape, F32)
@@ -319,7 +349,7 @@
             stride=1,
             stride_axis=0,
         )[:, :seq]
-        scores = dot_tn(qkv[1, part, :], qkv[0, part, :]) + bias
+        scores = dot_tn(qkv[1, part, :], qkv[0, part, :]) + jnp.transpose(bias)
         scores = jnp.where(key_valid, scores, -1e30)
         exps = jnp.exp(scores - jnp.max(scores, axis=0, keepdims=True))
         prob = exps / jnp.sum(exps, axis=0, keepdims=True)
@@ -393,9 +423,6 @@
         right_own[base] = hidden
         right_own[base + 1] = grad_gate
         right_own[base + 2] = grad_up
-        right_copy(base, 0).start()
-        right_copy(base + 1, 1).start()
-        right_copy(base + 2, 1).start()
         for block in blocks_of(width, MROWS):
             out_acc[block, :] += dot_nt(wd[slot, block, :], hidden)
             grad_acc[block, :] += dot_nt(wg[slot, block, :], grad_gate) + dot_nt(
@@ -425,6 +452,10 @@
             precision=lax.Precision.HIGHEST,
             preferred_element_type=F32,
         )[0:1, :]
+
+    def put_small(row, line):
+        small[row : row + 1, :] = line[:, : cfg.half]
+        small[row + 1 : row + 2, : width - cfg.half] = line[:, cfg.half :]
 
     def norm_two_back():
         pair_grad.wait()
@@ -456,7 +487,7 @@
         build_left(grad_acc, 3)
         left_copy(3).start()
         mask = lane_mask((8, seq), 1)
-        small[1:2, :width] = lane_sums(mask, trans[:width, :])
+        put_small(2, lane_sums(mask, trans[:width, :]))
 
     def attention_back():
         grad_att = dot(wo[core], grad_branch[...]).astype(BF)
@@ -476,17 +507,16 @@
             grad_qkv[1, part, :] = dot_nt(qkv[0, part, :], grad_scores).astype(BF)
             grad_qkv[2, part, :] = dot_nt(grad_mixed, prob.astype(BF)).astype(BF)
             flipped = jnp.concatenate(
-                [dot(flip, grad_scores), jnp.zeros((seq, seq), F32)], axis=1
+                [dot(grad_scores, flip), jnp.zeros((seq, seq), F32)], axis=1
             )
             skewed = pltpu.roll(flipped, 0, 1, stride=1, stride_axis=0)
-            small[2 + head : 3 + head, : 2 * seq] = jnp.sum(skewed, axis=0, keepdims=True)
+            small[4 + head : 5 + head, : 2 * seq] = jnp.sum(skewed, axis=0, keepdims=True)
         joined = jnp.concatenate(
             [grad_qkv[...].reshape(3 * hw, seq), attended[core]], axis=0
         ).astype(F32)
         for index in range(cfg.chunks - cfg.ff_total):
             chunk = cfg.ff_total + index
             right_own[chunk] = jnp.transpose(joined[index * CW : (index + 1) * CW, :]).astype(BF)
-            right_copy(chunk, 1).start()
 
     def norm_one_sums():
         for block in blocks_of(width, 128):
@@ -538,24 +568,17 @@
             return carry
 
         lax.fori_loop(0, steps, last_rows, 0)
-        small[0:1, :width] = lane_sums(jnp.ones((8, rows), F32), trans[:width, :rows])
+        put_small(0, lane_sums(jnp.ones((8, rows), F32), trans[:width, :rows]))
         small_copy(0).start()
 
     def small_stage(k):
         small_copy(k).wait()
         if k == cfg.bits:
             row = lax.broadcasted_iota(jnp.int32, small.shape, 0)
-            small_out[...] = small[...] + jnp.where(row < 2, small_in[k], 0.0)
+            small_out[...] = small[...] + jnp.where(row < 4, small_in[k], 0.0)
         else:
             small[...] = small[...] + small_in[k]
             small_copy(k + 1).start()
-
-    def chunk_kind(chunk):
-        tail_part = lax.div(chunk, cfg.ff_total)
-        kind = lax.rem(chunk, 3)
-        which = (1 - tail_part) * lax.div(kind + 1, 2) + 2 * tail_part
-        y_first = 1 - lax.div(2 - which, 2)
-        return which, y_first
 
     def stage_copy(k, chunk, target):
         slot = lax.rem(chunk, SLOTS)
@@ -568,30 +591,35 @@
         )
 
     def stage_target(k, chunk):
-        if k > 0:
-            return peer[k + 1]
-        y_first = chunk_kind(chunk)[1]
-        return y_first * peer[0] + (1 - y_first) * peer[1]
+        return pick(chunk, k + 1, peer)
 
     def form(chunk):
-        which, y_first = chunk_kind(chunk)
+        tail_part = lax.div(chunk, cfg.ff_total)
+        which = (1 - tail_part) * lax.div(lax.rem(chunk, 3) + 1, 2) + 2 * tail_part
         slot = lax.rem(chunk, SLOTS)
-        first_bit = y_first * bit[1] + (1 - y_first) * bit[0]
-        second_bit = y_first * bit[0] + (1 - y_first) * bit[1]
+        first_bit = pick(chunk, 0, bit)
+        second_bit = pick(chunk, 1, bit)
 
         @pl.when(chunk == 0)
         def _():
-            left_copy(0).wait()
+            left_pass(0)
+            left_pass(2)
+            left_share(0).wait()
 
         @pl.when(chunk == 1)
         def _():
-            left_copy(1).wait()
+            left_pass(1)
+            left_share(1).wait()
 
         @pl.when(chunk == cfg.ff_total)
         def _():
-            left_copy(2).wait()
-
-        right_copy(chunk, 0).wait()
+            left_share(2).wait()
+
+        @pl.when(chunk == cfg.chunks - 2)
+        def _():
+            left_pass(3)
+
+        right_copy(chunk).wait()
 
         def product(left, quarter):
             return dot(left_own[left, first_bit, quarter], right_own[chunk]) + dot(
@@ -606,7 +634,7 @@
 
         @pl.when(chunk == cfg.chunks - 1)
         def _():
-            left_copy(3).wait()
+            left_share(3).wait()
             split = lax.broadcasted_iota(jnp.int32, (cfg.quarter, CW), 1) < CW - hw
 
             def mixed(quarter):
@@ -633,7 +661,7 @@
 
             return
         half = cfg.stage_rows[k]
-        mine = bit[k + 1]
+        mine = pick(chunk, k + 1, bit)
 
         def total(which):
             part = pl.ds(pl.multiple_of(which * half, 16), half)
@@ -643,10 +671,12 @@
         stage_copy(k, chunk, stage_target(k, chunk)).start()
         stage_own[k][slot] = total(mine)
 
-    last_ff = 3 * (cfg.ff_chunks - 1)
+    last_ff = FF_TICKS * (cfg.ff_chunks - 1)
     pieces = [exchange_sums, norm_two_back, attention_back, norm_one_sums, finish_rows]
-    pieces += [functools.partial(small_stage, k) for k in range(cfg.bits + 1)]
-    ticks = max(LAG + cfg.chunks + GAP * stages, last_ff + len(pieces))
+    pieces = [(last_ff + index, piece) for index, piece in enumerate(pieces)]
+    for k in range(cfg.bits + 1):
+        pieces.append((pieces[-1][0] + SMALL_GAP, functools.partial(small_stage, k)))
+    ticks = max(LAG + cfg.chunks + GAP * stages, pieces[-1][0] + 1)
 
     def tick(t, carry):
         for k in range(stages, 0, -1):
@@ -662,15 +692,19 @@
         def _():
             form(new)
 
-        @pl.when(jnp.logical_and(lax.rem(t, 3) == 0, t <= last_ff))
+        @pl.when(jnp.logical_and(lax.rem(t, FF_TICKS) == 0, t <= last_ff))
         def _():
-            feed_forward(lax.div(t, 3))
-
-        for index, piece in enumerate(pieces):
-
-            @pl.when(t == last_ff + index)
+            feed_forward(lax.div(t, FF_TICKS))
+
+        for when, piece in pieces:
+
+            @pl.when(t == when)
             def _(piece=piece):
                 piece()
+
+        @pl.when(t < cfg.chunks)
+        def _():
+            right_copy(t).start()
 
         return carry
 
@@ -680,6 +714,70 @@
     for part, ref in enumerate((query_out, key_out, value_out)):
         ref[...] = flat[: cfg.shard, part * hw : (part + 1) * hw]
     output_out[...] = jnp.transpose(flat[:, 3 * hw :])[:, : cfg.shard]
+
+
+def finish_kernel(
+    cfg,
+    layer_in,
+    grad_in,
+    query_in,
+    key_in,
+    value_in,
+    output_in,
+    ff_in,
+    small,
+    bucket_ids,
+    layer_out,
+    grad_out,
+    gain_one,
+    query_out,
+    key_out,
+    value_out,
+    output_out,
+    bias_out,
+    gain_two,
+    gate_out,
+    up_out,
+    down_out,
+    *rest,
+):
+    pairs = [
+        (ff_in.at[0], down_out),
+        (ff_in.at[1], gate_out),
+        (ff_in.at[2], up_out),
+        (layer_in, layer_out),
+        (grad_in, grad_out),
+        (query_in, query_out),
+        (key_in, key_out),
+        (value_in, value_out),
+        (output_in, output_out),
+    ]
+    buffers, (load_sem, store_sem) = rest[:-2], rest[-2:]
+    loads, stores = [], []
+    for index, ((src, dst), buffer) in enumerate(zip(pairs, buffers)):
+        loads.append(pltpu.make_async_copy(src, buffer, load_sem.at[index]))
+        stores.append(pltpu.make_async_copy(buffer, dst, store_sem.at[index]))
+    for load in loads:
+        load.start()
+    for load, store in zip(loads, stores):
+        load.wait()
+        store.start()
+    for row, gain in ((0, gain_one), (2, gain_two)):
+        line = jnp.concatenate([small[row : row + 1, :], small[row + 1 : row + 2, :]], axis=1)
+        gain[...] = line[:, : cfg.width].reshape(cfg.width)
+    offsets = bucket_ids.shape[0]
+    bucket = lax.broadcasted_iota(jnp.int32, (cfg.buckets, offsets), 0)
+    onehot = (bucket_ids[...].reshape(1, offsets) == bucket).astype(F32)
+    sums = lax.dot_general(
+        small[:, :offsets],
+        onehot,
+        (((1,), (1,)), ((), ())),
+        precision=lax.Precision.HIGHEST,
+        preferred_element_type=F32,
+    )
+    bias_out[...] = sums[4 : 4 + cfg.heads, :]
+    for store in stores:
+        store.wait()
 
 
 def shards(
@@ -709,7 +807,7 @@
     any_spec = pl.BlockSpec(memory_space=pl.ANY)
     vmem = pl.BlockSpec(memory_space=pltpu.VMEM)
     smem = pl.BlockSpec(memory_space=pltpu.SMEM)
-    small_shape = (8, cfg.wide)
+    small_shape = (8, cfg.half)
     scratch = [
         pltpu.VMEM((2, width, rows), BF),
         pltpu.VMEM((2, width, rows), BF),
@@ -745,6 +843,7 @@
         pltpu.VMEM(small_shape, F32),
         pltpu.VMEM((cfg.bits + 1,) + small_shape, F32),
         pltpu.VMEM((cfg.chunks - cfg.ff_total, cfg.shard_pad, CW), F32),
+        pltpu.VMEM((1, 2 * seq), jnp.int32),
     ]
     scratch += [pltpu.VMEM((SLOTS, size, CW), F32) for size in cfg.stage_rows]
     scratch += [pltpu.VMEM((SLOTS, size, CW), BF) for size in cfg.stage_rows]
@@ -757,6 +856,8 @@
         dma((7,)),
         dma((4,)),
         dma((4,)),
+        dma((4,)),
+        dma((4,)),
         dma((cfg.chunks,)),
         dma((cfg.chunks,)),
         dma((stages, SLOTS)),
@@ -764,9 +865,6 @@
         dma((cfg.bits + 1,)),
         dma((cfg.bits + 1,)),
     ]
-    reversed_ids = jnp.pad(
-        jnp.flip(bucket_ids), (0, 2 * seq - bucket_ids.shape[0]), constant_values=-1
-    )
     (
         layer_out,
         input_grad,
@@ -815,41 +913,75 @@
         ),
     )(
         hidden_in.T,
-        attention_gain.reshape(1, width),
+        attention_gain,
         query_weight.T,
         key_weight.T,
         value_weight.T,
         output_weight,
         position_bias.T,
-        feedforward_gain.reshape(1, width),
+        feedforward_gain,
         gate_weight,
         up_weight,
         down_weight.T,
         cotangent.T,
         item_lengths,
         item_group,
-        reversed_ids.reshape(1, -1),
+        bucket_ids,
     )
-    onehot = (
-        jnp.flip(bucket_ids)[None, :] == jnp.arange(buckets, dtype=jnp.int32)[:, None]
-    ).astype(F32)
-    diagonals = small_sum[2 : 2 + cfg.heads, : bucket_ids.shape[0]]
-    bias_total = lax.dot_general(
-        onehot, diagonals, (((1,), (1,)), ((), ())), precision=lax.Precision.HIGHEST
-    )
-    return (
-        layer_out.T,
-        input_grad.T,
-        small_sum[0, :width],
+    def like(array):
+        return jax.ShapeDtypeStruct(array.shape, array.dtype)
+
+    one_ff = jax.ShapeDtypeStruct((shard, hidden), F32)
+    outs = pl.pallas_call(
+        functools.partial(finish_kernel, cfg),
+        out_shape=[
+            like(layer_out),
+            like(input_grad),
+            like(attention_gain),
+            like(query_sum),
+            like(key_sum),
+            like(value_sum),
+            like(output_sum),
+            jax.ShapeDtypeStruct((cfg.heads, buckets), F32),
+            like(feedforward_gain),
+            one_ff,
+            one_ff,
+            one_ff,
+        ],
+        in_specs=[any_spec] * 7 + [vmem, vmem],
+        out_specs=[any_spec] * 2 + [vmem] + [any_spec] * 4 + [vmem] * 2 + [any_spec] * 3,
+        scratch_shapes=[
+            pltpu.VMEM(array.shape, F32)
+            for array in (one_ff,) * 3
+            + (layer_out, input_grad, query_sum, key_sum, value_sum, output_sum)
+        ]
+        + [dma((9,)), dma((9,))],
+        compiler_params=pltpu.CompilerParams(vmem_limit_bytes=16 * 1024 * 1024),
+    )(
+        layer_out,
+        input_grad,
         query_sum,
         key_sum,
         value_sum,
         output_sum,
-        bias_total,
-        small_sum[1, :width],
-        ff_sum[1],
-        ff_sum[2],
-        ff_sum[0].T,
+        ff_sum,
+        small_sum,
+        bucket_ids,
+    )
+    layer_out, input_grad, gain_one, query, key, value, output, bias, gain_two, gate, up, down = outs
+    return (
+        layer_out.T,
+        input_grad.T,
+        gain_one,
+        query,
+        key,
+        value,
+        output,
+        bias.T,
+        gain_two,
+        gate,
+        up,
+        down.T,
     )
 
 

time: 164 us -> 141 us (0.86)
  Pallas kernels: 147 us -> 131 us
  local copies, waits for them, and re-layouts: 13.9 us -> 8.12 us
    pallas_call x1, Pallas kernels: 147 us -> 127 us  [shards(): pl.pallas_call(functools.partial(layer_kernel, cfg), out_shape=[jax.Shape...]
    pallas_call x0 -> x1, Pallas kernels: none -> 4.77 us  [shards(): pl.pallas_call(functools.partial(finish_kernel, cfg), out_shape=[like(lay...]
    transpose x1 -> x0, local copies, waits for them, and re-layouts: 2.86 us -> none  [shards(): ff_sum[0]]
    reshape x2 -> x0, local copies, waits for them, and re-layouts: 2.59 us -> none  [the longest x1 1.29 us: shards(): attention_gain.reshape(1, width)]
    unnamed x18, local copies, waits for them, and re-layouts: 6.34 us -> 8.12 us
where the time goes in v3:
time: 141 us; the launch traced here: 140 us
  Pallas kernels  131 us (93%)
  local copies, waits for them, and re-layouts  8.12 us (6%)
    pallas_call x1, Pallas kernels, shards(): pl.pallas_call(functools.partial(layer_kernel, cfg), out_shape=[jax.Shape...  127 us
    unnamed x18, local copies, waits for them, and re-layouts  8.12 us
    pallas_call x1, Pallas kernels, shards(): pl.pallas_call(functools.partial(finish_kernel, cfg), out_shape=[like(lay...  4.77 us

profile of v3, /device:TPU:0, one launch (start us, length us, event | category | flops | bytes accessed | tf_op | source)
XLA Modules:
  0.0 140.2 jit_solution(7471757842383854040)
XLA Ops:
  0.7 0.0 copy-start.8
  0.7 126.6 %shard_map.238 = (f32[1472,128]{1,0:T(8,128)}, f32[1472,128]{1,0:T(8,128)}, f32[8,768]{1,0:T(8,128)}, f32[3,92,1792]{2,1,0:T(8,128)}, f32[92,192]{1,0:T(8,128)},...) custom-call(bf16[1472,128]{1,0:T(8,128)(2,1)} %bitcast.18, f32[1472]{0:T(1024)} %gain_one.1, ...), custom_call_target="tpu_custom_call" | custom-call | flops 14000000000 | bytes 24000000 | tf_op jit(solution)/shard_map/pallas_call | solution.py:877
  127.3 0.0 copy-done.8
  127.3 0.0 copy-start
  127.3 1.6 %copy-done = f32[3,92,1792]{2,1,0:T(8,128)S(1)} copy-done((f32[3,92,1792]{2,1,0:T(8,128)S(1)}, f32[3,92,1792]{2,1,0:T(8,128)}, u32[]{:S(2)}) %copy-start) | copy-done | bytes 1978392
  128.9 0.0 copy-start.1
  128.9 1.1 copy-done.1
  130.0 0.0 copy-start.2
  130.0 1.1 copy-done.2
  131.1 0.0 copy-start.3
  131.1 0.9 copy-done.3
  132.0 0.0 copy-start.4
  132.0 0.9 copy-done.4
  132.9 0.0 copy-start.5
  132.9 0.9 copy-done.5
  133.8 0.0 copy-start.6
  133.8 0.9 copy-done.6
  134.7 0.0 copy-start.7
  134.7 0.7 copy-done.7
  135.5 4.8 %shard_map.239 = (f32[1472,128]{1,0:T(8,128)}, f32[1472,128]{1,0:T(8,128)}, f32[1472]{0:T(1024)}, f32[92,192]{1,0:T(8,128)}, f32[92,192]{1,0:T(8,128)}, /*index=...) custom-call(f32[1472,128]{1,0:T(8,128)S(1)} %copy-done.1, ...), custom_call_target="tpu_custom_call" | custom-call | tf_op jit(solution)/shard_map/pallas_call | solution.py:935
Async XLA Ops:
  0.7 126.7 %copy-start.8 = (s32[511]{0:T(512)S(1)}, s32[511]{0:T(512)}, u32[]{:S(2)}) copy-start(s32[511]{0:T(512)} %bucket_ids.3) | copy-start | bytes 6136
  127.3 1.6 %copy-start = (f32[3,92,1792]{2,1,0:T(8,128)S(1)}, f32[3,92,1792]{2,1,0:T(8,128)}, u32[]{:S(2)}) copy-start(f32[3,92,1792]{2,1,0:T(8,128)} %get-tuple-element.38.ff_in) | copy-start | bytes 5935108
  128.9 1.1 copy-start.1
  130.0 1.1 copy-start.2
  131.1 0.9 copy-start.3
  132.0 0.9 copy-start.4
  132.9 0.9 copy-start.5
  133.8 0.9 copy-start.6
  134.7 0.7 copy-start.7

commit v4 on v3

--- a/solution.py
+++ b/solution.py
@@ -11,12 +11,13 @@
 DKV = 64
 CW = 256
 EPS = 1e-06
-LAG = 3
-GAP = 3
-SLOTS = 4
+LAG = 5
+GAP = 4
+SLOTS = GAP + 1
 FF_TICKS = 2
+LEAD = 1
 SMALL_GAP = 3
-AXES = ((0, 1, 2), (1, 0, 2), (2, 1, 0), (2, 1, 0))
+AXES = ((0, 1, 2), (1, 0, 2), (2, 0, 1), (2, 1, 0), (2, 1, 0))
 STEP = 64
 MROWS = 368
 BF = jnp.bfloat16
@@ -117,7 +118,6 @@
     right_in,
     out_acc,
     grad_acc,
-    grad_send,
     grad_in,
     part_send,
     part_in,
@@ -131,6 +131,7 @@
     ids_row,
     *rest,
 ):
+    grad_send = normed_one
     stages = cfg.stages
     stage_own = rest[:stages]
     stage_send = rest[stages : 2 * stages]
@@ -267,12 +268,17 @@
         left_share(which).start()
 
     def pick(chunk, level, values):
-        ks = [cfg.orders[which][level] for which in range(3)]
-        if ks[0] == ks[1] == ks[2]:
+        ks = [cfg.orders[which][level] for which in range(4)]
+        if len(set(ks)) == 1:
             return values[ks[0]]
         tail_part = lax.div(chunk, cfg.ff_total)
-        hidden_part = (1 - tail_part) * (1 - lax.div(lax.rem(chunk, 3) + 1, 2))
-        parts = (hidden_part, 1 - tail_part - hidden_part, tail_part)
+        kind = lax.rem(chunk, 3)
+        parts = (
+            (1 - tail_part) * lax.div((1 - kind) * (2 - kind), 2),
+            (1 - tail_part) * kind * (2 - kind),
+            (1 - tail_part) * lax.div(kind * (kind - 1), 2),
+            tail_part,
+        )
         return sum(part * values[k] for part, k in zip(parts, ks))
 
     def right_copy(chunk):
@@ -357,8 +363,8 @@
         attended[core, part, :] = dot(qkv[2, part, :], prob.astype(BF)).astype(BF)
     pair_att.start()
 
-    build_left(trans, 2)
-    left_copy(2).start()
+    build_left(trans, 3)
+    left_copy(3).start()
     loads[1].wait()
     pair_cot.wait()
     row_valid = lax.broadcasted_iota(jnp.int32, (step_rows, seq), 1) < group_len
@@ -397,6 +403,8 @@
     lax.fori_loop(0, steps, norm_two_rows, 0)
     build_left(trans, 1)
     left_copy(1).start()
+    build_left(trans, 2)
+    left_copy(2).start()
     for block in blocks_of(width, 128):
         normed_two[:, block] = jnp.transpose(trans[block, :]).astype(BF)
     small[...] = jnp.zeros_like(small)
@@ -484,8 +492,8 @@
             return carry
 
         lax.fori_loop(0, steps, back_rows, 0)
-        build_left(grad_acc, 3)
-        left_copy(3).start()
+        build_left(grad_acc, 4)
+        left_copy(4).start()
         mask = lane_mask((8, seq), 1)
         put_small(2, lane_sums(mask, trans[:width, :]))
 
@@ -595,7 +603,7 @@
 
     def form(chunk):
         tail_part = lax.div(chunk, cfg.ff_total)
-        which = (1 - tail_part) * lax.div(lax.rem(chunk, 3) + 1, 2) + 2 * tail_part
+        which = (1 - tail_part) * lax.rem(chunk, 3) + 3 * tail_part
         slot = lax.rem(chunk, SLOTS)
         first_bit = pick(chunk, 0, bit)
         second_bit = pick(chunk, 1, bit)
@@ -603,21 +611,26 @@
         @pl.when(chunk == 0)
         def _():
             left_pass(0)
+            left_pass(1)
             left_pass(2)
             left_share(0).wait()
 
         @pl.when(chunk == 1)
         def _():
-            left_pass(1)
+            left_pass(3)
             left_share(1).wait()
+
+        @pl.when(chunk == 2)
+        def _():
+            left_share(2).wait()
 
         @pl.when(chunk == cfg.ff_total)
         def _():
-            left_share(2).wait()
+            left_share(3).wait()
 
         @pl.when(chunk == cfg.chunks - 2)
         def _():
-            left_pass(3)
+            left_pass(4)
 
         right_copy(chunk).wait()
 
@@ -634,11 +647,11 @@
 
         @pl.when(chunk == cfg.chunks - 1)
         def _():
-            left_share(3).wait()
+            left_share(4).wait()
             split = lax.broadcasted_iota(jnp.int32, (cfg.quarter, CW), 1) < CW - hw
 
             def mixed(quarter):
-                return jnp.where(split, product(2, quarter), product(3, quarter))
+                return jnp.where(split, product(3, quarter), product(4, quarter))
 
             stage_send[0][slot] = mixed(1 - second_bit).astype(BF)
             stage_copy(0, chunk, stage_target(0, chunk)).start()
@@ -702,9 +715,15 @@
             def _(piece=piece):
                 piece()
 
-        @pl.when(t < cfg.chunks)
+        for early in range(LEAD):
+
+            @pl.when(t == 0)
+            def _(early=early):
+                right_copy(early).start()
+
+        @pl.when(t + LEAD < cfg.chunks)
         def _():
-            right_copy(t).start()
+            right_copy(t + LEAD).start()
 
         return carry
 
@@ -826,13 +845,12 @@
         pltpu.VMEM((cfg.heads, seq, seq), F32),
         pltpu.VMEM((2, hw, seq), BF),
         pltpu.VMEM((cfg.tall, seq), F32),
-        pltpu.VMEM((4, 2, 2, cfg.quarter, seq), BF),
-        pltpu.VMEM((4, 2, cfg.quarter, seq), BF),
+        pltpu.VMEM((len(AXES), 2, 2, cfg.quarter, seq), BF),
+        pltpu.VMEM((len(AXES), 2, cfg.quarter, seq), BF),
         pltpu.VMEM((cfg.chunks, seq, CW), BF),
         pltpu.VMEM((cfg.chunks, seq, CW), BF),
         pltpu.VMEM((width, seq), F32),
         pltpu.VMEM((cfg.tall, seq), F32),
-        pltpu.VMEM((width, seq), BF),
         pltpu.VMEM((width, seq), BF),
         pltpu.VMEM((width, rows), BF),
         pltpu.VMEM((width, rows), BF),
@@ -854,10 +872,10 @@
         dma((2, 3)),
         dma((7,)),
         dma((7,)),
-        dma((4,)),
-        dma((4,)),
-        dma((4,)),
-        dma((4,)),
+        dma((len(AXES),)),
+        dma((len(AXES),)),
+        dma((len(AXES),)),
+        dma((len(AXES),)),
         dma((cfg.chunks,)),
         dma((cfg.chunks,)),
         dma((stages, SLOTS)),
@@ -906,7 +924,7 @@
         out_specs=[vmem] * 8,
         scratch_shapes=scratch,
         compiler_params=pltpu.CompilerParams(
-            collective_id=0, has_side_effects=True, vmem_limit_bytes=60 * 1024 * 1024
+            collective_id=0, has_side_effects=True, vmem_limit_bytes=62 * 1024 * 1024
         ),
         cost_estimate=pl.CostEstimate(
             flops=14 * 10**9, bytes_accessed=24 * 10**6, transcendentals=10**6
@@ -956,7 +974,7 @@
             + (layer_out, input_grad, query_sum, key_sum, value_sum, output_sum)
         ]
         + [dma((9,)), dma((9,))],
-        compiler_params=pltpu.CompilerParams(vmem_limit_bytes=16 * 1024 * 1024),
+        compiler_params=pltpu.CompilerParams(vmem_limit_bytes=62 * 1024 * 1024),
     )(
         layer_out,
         input_grad,

time: 141 us -> 130 us (0.922)
  local copies, waits for them, and re-layouts: 8.12 us -> 0 us
  Pallas kernels: 131 us -> 129 us
    unnamed x18 -> x0, local copies, waits for them, and re-layouts: 8.12 us -> none
    pallas_call x1, Pallas kernels: 127 us -> 124 us  [shards(): pl.pallas_call(functools.partial(layer_kernel, cfg), out_shape=[jax.Shape...]
where the time goes in v4:
time: 130 us; the launch traced here: 129 us
  Pallas kernels  129 us (99%)
    pallas_call x1, Pallas kernels, shards(): pl.pallas_call(functools.partial(layer_kernel, cfg), out_shape=[jax.Shape...  124 us
    pallas_call x1, Pallas kernels, shards(): pl.pallas_call(functools.partial(finish_kernel, cfg), out_shape=[like(lay...  4.52 us

profile of v4, /device:TPU:0, one launch (start us, length us, event | category | flops | bytes accessed | tf_op | source)
XLA Modules:
  0.0 129.3 jit_solution(7368605798000911923)
XLA Ops:
  0.6 124.2 %shard_map.238 = (f32[1472,128]{1,0:T(8,128)}, f32[1472,128]{1,0:T(8,128)}, f32[8,768]{1,0:T(8,128)}, f32[3,92,1792]{2,1,0:T(8,128)}, f32[92,192]{1,0:T(8,128)},...) custom-call(bf16[1472,128]{1,0:T(8,128)(2,1)} %bitcast.18, f32[1472]{0:T(1024)} %gain_one.1, ...), custom_call_target="tpu_custom_call" | custom-call | flops 14000000000 | bytes 24000000 | tf_op jit(solution)/shard_map/pallas_call | solution.py:895
  124.8 4.5 %shard_map.239 = (f32[1472,128]{1,0:T(8,128)}, f32[1472,128]{1,0:T(8,128)}, f32[1472]{0:T(1024)}, f32[92,192]{1,0:T(8,128)}, f32[92,192]{1,0:T(8,128)}, /*index=...) custom-call(f32[1472,128]{1,0:T(8,128)} %get-tuple-element.32.layer_, ...), custom_call_target="tpu_custom_call" | custom-call | tf_op jit(solution)/shard_map/pallas_call | solution.py:953

commit v5 on v3

--- a/solution.py
+++ b/solution.py
@@ -11,12 +11,15 @@
 DKV = 64
 CW = 256
 EPS = 1e-06
-LAG = 3
-GAP = 3
-SLOTS = 4
-FF_TICKS = 2
+AXES = ((1, 0, 2), (1, 2, 0), (2, 1, 0), (2, 1, 0), (2, 0, 1), (2, 1, 0), (1, 0, 2), (2, 1, 0))
+TOGETHER = (2, 3, 2)
+FF_TICKS = (0, 1, 4, 7, 8, 10, 12)
+RING_BLOCKS = 5
+LAG = 0
+GAP = 4
+SLOTS = GAP + 1
+RING = 3 * RING_BLOCKS
 SMALL_GAP = 3
-AXES = ((0, 1, 2), (1, 0, 2), (2, 1, 0), (2, 1, 0))
 STEP = 64
 MROWS = 368
 BF = jnp.bfloat16
@@ -43,6 +46,22 @@
 
 def fold(block):
     return jnp.sum(block.reshape(block.shape[0] // 8, 8, block.shape[1]), axis=0)
+
+
+def lookup(table, index):
+    bits = max(table).bit_length()
+    if bits == 0:
+        return 0 * index
+    per = 30 // bits
+    words = [
+        sum(value << (bits * place) for place, value in enumerate(table[begin : begin + per]))
+        for begin in range(0, len(table), per)
+    ]
+    word = jnp.int32(words[0])
+    for place in range(1, len(words)):
+        word = jnp.where(index >= place * per, words[place], word)
+    shifted = lax.shift_right_logical(word, bits * lax.rem(index, per))
+    return lax.rem(shifted, 1 << bits)
 
 
 class Sizes:
@@ -66,7 +85,15 @@
         self.stages = len(self.stage_rows)
         self.half = -(-width // 256) * 128
         self.tall = width + self.shard_pad
-        self.orders = [axes + tuple(range(3, self.bits)) for axes in AXES]
+        self.eighth = self.quarter // 2
+        self.order = []
+        begin = 0
+        for count in TOGETHER:
+            self.order += [3 * (begin + f) + kind for kind in range(3) for f in range(count)]
+            begin += count
+        self.order += range(self.ff_total, self.chunks)
+        self.near = sorted({axes[0] for axes in AXES[: self.ff_chunks]})
+        self.first_use = [[axes[0] for axes in AXES].index(axis) for axis in self.near]
 
 
 def layer_kernel(
@@ -113,11 +140,11 @@
     trans,
     left_own,
     left_in,
+    near_rows,
     right_own,
     right_in,
     out_acc,
     grad_acc,
-    grad_send,
     grad_in,
     part_send,
     part_in,
@@ -131,6 +158,7 @@
     ids_row,
     *rest,
 ):
+    grad_send = normed_one
     stages = cfg.stages
     stage_own = rest[:stages]
     stage_send = rest[stages : 2 * stages]
@@ -144,6 +172,10 @@
         left_recv_sem,
         share_send_sem,
         share_recv_sem,
+        near_send_sem,
+        near_recv_sem,
+        pass_send_sem,
+        pass_recv_sem,
         right_send_sem,
         right_recv_sem,
         stage_send_sem,
@@ -159,6 +191,7 @@
     peer = [me + (1 - 2 * bit[k]) * (1 << k) for k in range(cfg.bits)]
     sibling = (me, 1 - core)
     own_lanes = pl.ds(pl.multiple_of(core * rows, rows), rows)
+    own_rows = own_lanes
     other_lanes = pl.ds(pl.multiple_of((1 - core) * rows, rows), rows)
 
     def send(src, dst, send_sem, recv_sem, target):
@@ -200,6 +233,15 @@
             gains[index, block, :] = jnp.transpose(
                 jnp.broadcast_to(line[:, block], (128, size))
             )
+    group_len = jnp.int32(0)
+    for item in range(lengths.shape[0]):
+        group_len = group_len + jnp.where(groups[item] == me, lengths[item], 0)
+
+    loads[1].wait()
+    lane_valid = lax.broadcasted_iota(jnp.int32, (1, rows), 1) + core * rows < group_len
+    for block in blocks_of(width, 128):
+        part = jnp.where(lane_valid, cot_raw[core, block, :].astype(F32), 0.0)
+        cot[own_rows, block] = jnp.transpose(part).astype(BF)
     pl.semaphore_wait(barrier, cfg.bits + 1)
 
     pair_hid = send(
@@ -209,9 +251,36 @@
         cot_hbm, cot_raw.at[core], pair_send_sem.at[1], pair_recv_sem.at[1], sibling
     )
     pair_wo = send(wo_hbm, wo.at[core], pair_send_sem.at[2], pair_recv_sem.at[2], sibling)
+    pair_rows = send(
+        cot.at[own_rows], cot.at[own_rows], pair_send_sem.at[7], pair_recv_sem.at[7], sibling
+    )
+
+    natural = (cot, normed_two)
+
+    def near_copy(near, which):
+        return send(
+            natural[which].at[own_rows],
+            near_rows.at[near, which, own_rows],
+            near_send_sem.at[near, which],
+            near_recv_sem.at[near, which],
+            (peer[cfg.near[near]], core),
+        )
+
+    def near_pass(near, which):
+        return send(
+            near_rows.at[near, which, own_rows],
+            near_rows.at[near, which, own_rows],
+            pass_send_sem.at[near, which],
+            pass_recv_sem.at[near, which],
+            sibling,
+        )
+
     pair_hid.start()
     pair_cot.start()
     pair_wo.start()
+    pair_rows.start()
+    for near in range(len(cfg.near)):
+        near_copy(near, 0).start()
     pair_att = send(
         attended.at[core], attended.at[core], pair_send_sem.at[3], pair_recv_sem.at[3], sibling
     )
@@ -223,40 +292,49 @@
         for load in weight_loads(slot, slot):
             load.start()
 
-    group_len = jnp.int32(0)
-    for item in range(lengths.shape[0]):
-        group_len = group_len + jnp.where(groups[item] == me, lengths[item], 0)
+    def place_of(index):
+        place = 0
+        for k in range(3, cfg.bits):
+            place = 2 * place + ((index >> k) & 1)
+        return slice(place * cfg.shard_pad, (place + 1) * cfg.shard_pad)
+
+    def shard_of(source, index):
+        return source[index * cfg.shard : index * cfg.shard + cfg.shard_pad, :].astype(BF)
 
     def build_left(source, which):
-        order = cfg.orders[which]
         for index in range(cfg.dp):
-            bits = [(index >> k) & 1 for k in order]
-            place = 0
-            for value in bits[2:]:
-                place = 2 * place + value
-            block = source[index * cfg.shard : index * cfg.shard + cfg.shard_pad, :]
-            left_own[
-                which,
-                bits[0],
-                bits[1],
-                place * cfg.shard_pad : (place + 1) * cfg.shard_pad,
-                :,
-            ] = block.astype(BF)
+            left_own[which, index & 7, place_of(index), :] = shard_of(source, index)
+
+    def adopt(near, which):
+        near_copy(near, which).wait()
+        near_pass(near, which).start()
+        near_pass(near, which).wait()
+        axis = cfg.near[near]
+        high, low = (k for k in (2, 1, 0) if k != axis)
+        for block in blocks_of(width, 128):
+            trans[block, :] = jnp.transpose(near_rows[near, which, :, block].astype(F32))
+        for value in range(2):
+
+            @pl.when(bit[axis] == value)
+            def _(value=value):
+                for index in range(cfg.dp):
+                    if (index >> axis) & 1 == value:
+                        place = 2 * ((index >> high) & 1) + ((index >> low) & 1)
+                        left_in[near, which, place, place_of(index), :] = shard_of(trans, index)
 
     def left_copy(which):
-        first = cfg.orders[which][0]
         return send(
-            left_own.at[which, 1 - bit[first], core],
-            left_in.at[which, core],
+            left_own.at[2 + which, pl.ds(4 * (1 - bit[2]) + 2 * core, 2)],
+            left_in.at[len(cfg.near), which, pl.ds(2 * core, 2)],
             left_send_sem.at[which],
             left_recv_sem.at[which],
-            (peer[first], core),
+            (peer[2], core),
         )
 
     def left_share(which):
         return send(
-            left_in.at[which, core],
-            left_in.at[which, core],
+            left_in.at[len(cfg.near), which, pl.ds(2 * core, 2)],
+            left_in.at[len(cfg.near), which, pl.ds(2 * core, 2)],
             share_send_sem.at[which],
             share_recv_sem.at[which],
             sibling,
@@ -266,22 +344,27 @@
         left_copy(which).wait()
         left_share(which).start()
 
+    def block_of(chunk):
+        return lax.div(chunk, 3)
+
     def pick(chunk, level, values):
-        ks = [cfg.orders[which][level] for which in range(3)]
-        if ks[0] == ks[1] == ks[2]:
-            return values[ks[0]]
+        if level > 2:
+            return values[level]
+        k = lookup([axes[level] for axes in AXES], block_of(chunk))
+        parts = (lax.div((1 - k) * (2 - k), 2), k * (2 - k), lax.div(k * (k - 1), 2))
+        return sum(part * value for part, value in zip(parts, values))
+
+    def right_slot(chunk):
         tail_part = lax.div(chunk, cfg.ff_total)
-        hidden_part = (1 - tail_part) * (1 - lax.div(lax.rem(chunk, 3) + 1, 2))
-        parts = (hidden_part, 1 - tail_part - hidden_part, tail_part)
-        return sum(part * values[k] for part, k in zip(parts, ks))
-
-    def right_copy(chunk):
+        return (1 - tail_part) * lax.rem(chunk, RING) + tail_part * (RING + chunk - cfg.ff_total)
+
+    def right_copy(index):
         return send(
-            right_own.at[chunk],
-            right_in.at[chunk],
-            right_send_sem.at[chunk],
-            right_recv_sem.at[chunk],
-            (pick(chunk, 0, peer), core),
+            right_own.at[RING + index],
+            right_in.at[RING + index],
+            right_send_sem.at[index],
+            right_recv_sem.at[index],
+            (peer[2], core),
         )
 
     for scratch in (trans, grad_acc):
@@ -358,9 +441,8 @@
     pair_att.start()
 
     build_left(trans, 2)
-    left_copy(2).start()
-    loads[1].wait()
     pair_cot.wait()
+    pair_rows.wait()
     row_valid = lax.broadcasted_iota(jnp.int32, (step_rows, seq), 1) < group_len
 
     def mask_rows(step, carry):
@@ -370,9 +452,6 @@
 
     lax.fori_loop(0, steps, mask_rows, 0)
     build_left(trans, 0)
-    left_copy(0).start()
-    for block in blocks_of(width, 128):
-        cot[:, block] = jnp.transpose(trans[block, :]).astype(BF)
 
     loads[5].wait()
     pair_wo.wait()
@@ -395,46 +474,59 @@
         return carry
 
     lax.fori_loop(0, steps, norm_two_rows, 0)
-    build_left(trans, 1)
-    left_copy(1).start()
     for block in blocks_of(width, 128):
         normed_two[:, block] = jnp.transpose(trans[block, :]).astype(BF)
+    for near in range(len(cfg.near)):
+        near_copy(near, 1).start()
+    build_left(trans, 1)
     small[...] = jnp.zeros_like(small)
 
     def feed_forward(chunk):
         slot = lax.rem(chunk, 2)
         for load in weight_loads(chunk, slot):
             load.wait()
-        normed = normed_two[...]
-        gate = dot(normed, wg[slot])
-        up = dot(normed, wu[slot])
-        grad_hidden = dot(cot[...], wd[slot])
-        square = gate * gate
-        tanh = jnp.tanh(GELU_C * (gate + 0.044715 * (square * gate)))
-        half = 0.5 * (1.0 + tanh)
-        gelu = gate * half
-        slope = half + (0.5 * GELU_C) * gate * (1.0 - tanh * tanh) * (
-            1.0 + (3 * 0.044715) * square
-        )
-        hidden = (gelu * up).astype(BF)
-        grad_gate = (grad_hidden * up * slope).astype(BF)
-        grad_up = (grad_hidden * gelu).astype(BF)
-        base = 3 * chunk
-        right_own[base] = hidden
-        right_own[base + 1] = grad_gate
-        right_own[base + 2] = grad_up
+        first = lax.rem(3 * chunk, RING)
+
+        def activations(normed, grad_rows, target):
+            gate = dot(normed, wg[slot])
+            up = dot(normed, wu[slot])
+            grad_hidden = dot(grad_rows, wd[slot])
+            square = gate * gate
+            tanh = jnp.tanh(GELU_C * (gate + 0.044715 * (square * gate)))
+            half = 0.5 * (1.0 + tanh)
+            gelu = gate * half
+            slope = half + (0.5 * GELU_C) * gate * (1.0 - tanh * tanh) * (
+                1.0 + (3 * 0.044715) * square
+            )
+            target[first] = (gelu * up).astype(BF)
+            target[first + 1] = (grad_hidden * up * slope).astype(BF)
+            target[first + 2] = (grad_hidden * gelu).astype(BF)
+
+        activations(normed_two[...], cot[...], right_own)
+        hidden, grad_gate, grad_up = (right_own[first + kind] for kind in range(3))
         for block in blocks_of(width, MROWS):
             out_acc[block, :] += dot_nt(wd[slot, block, :], hidden)
             grad_acc[block, :] += dot_nt(wg[slot, block, :], grad_gate) + dot_nt(
                 wu[slot, block, :], grad_up
             )
 
+        for near, use in enumerate(cfg.first_use):
+
+            @pl.when(chunk == use)
+            def _(near=near):
+                adopt(near, 0)
+                adopt(near, 1)
+
+        near = lookup([cfg.near.index(axes[0]) for axes in AXES[: cfg.ff_chunks]], chunk)
+        activations(near_rows[near, 1], near_rows[near, 0], right_in)
+
         @pl.when(chunk < cfg.ff_chunks - 2)
         def _():
             for load in weight_loads(chunk + 2, slot):
                 load.start()
 
     def exchange_sums():
+        left_copy(0).start()
         grad_send[...] = grad_acc[:width, :].astype(BF)
         pair_grad.start()
         part_send[...] = out_acc[:, other_lanes].astype(BF)
@@ -485,7 +577,7 @@
 
         lax.fori_loop(0, steps, back_rows, 0)
         build_left(grad_acc, 3)
-        left_copy(3).start()
+        left_copy(1).start()
         mask = lane_mask((8, seq), 1)
         put_small(2, lane_sums(mask, trans[:width, :]))
 
@@ -515,8 +607,10 @@
             [grad_qkv[...].reshape(3 * hw, seq), attended[core]], axis=0
         ).astype(F32)
         for index in range(cfg.chunks - cfg.ff_total):
-            chunk = cfg.ff_total + index
-            right_own[chunk] = jnp.transpose(joined[index * CW : (index + 1) * CW, :]).astype(BF)
+            right_own[RING + index] = jnp.transpose(
+                joined[index * CW : (index + 1) * CW, :]
+            ).astype(BF)
+            right_copy(index).start()
 
     def norm_one_sums():
         for block in blocks_of(width, 128):
@@ -580,8 +674,7 @@
             small[...] = small[...] + small_in[k]
             small_copy(k + 1).start()
 
-    def stage_copy(k, chunk, target):
-        slot = lax.rem(chunk, SLOTS)
+    def stage_copy(k, chunk, slot, target):
         return send(
             stage_send[k].at[slot],
             stage_in[k].at[chunk],
@@ -593,60 +686,82 @@
     def stage_target(k, chunk):
         return pick(chunk, k + 1, peer)
 
-    def form(chunk):
+    def form(chunk, slot):
         tail_part = lax.div(chunk, cfg.ff_total)
-        which = (1 - tail_part) * lax.div(lax.rem(chunk, 3) + 1, 2) + 2 * tail_part
-        slot = lax.rem(chunk, SLOTS)
-        first_bit = pick(chunk, 0, bit)
+        which = (1 - tail_part) * lax.div(lax.rem(chunk, 3) + 1, 2)
+        block = block_of(chunk)
+        spot = right_slot(chunk)
         second_bit = pick(chunk, 1, bit)
-
-        @pl.when(chunk == 0)
+        weights = [pick(chunk, level, (1, 2, 4)) for level in range(3)]
+        descending = lookup([int(axes[1] > axes[2]) for axes in AXES], block)
+        near_weights = 1 + descending, 2 - descending
+        begin = weights[0] * pick(chunk, 0, bit)
+
+        @pl.when(chunk == cfg.ff_total)
         def _():
             left_pass(0)
-            left_pass(2)
             left_share(0).wait()
 
-        @pl.when(chunk == 1)
+        @pl.when(chunk == cfg.chunks - 1)
         def _():
             left_pass(1)
             left_share(1).wait()
 
-        @pl.when(chunk == cfg.ff_total)
-        def _():
-            left_share(2).wait()
-
-        @pl.when(chunk == cfg.chunks - 2)
-        def _():
-            left_pass(3)
-
-        right_copy(chunk).wait()
-
-        def product(left, quarter):
-            return dot(left_own[left, first_bit, quarter], right_own[chunk]) + dot(
-                left_in[left, quarter], right_in[chunk]
+        for index in range(cfg.chunks - cfg.ff_total):
+
+            @pl.when(chunk == cfg.ff_total + index)
+            def _(index=index):
+                right_copy(index).wait()
+
+        def product(own, near, second, third):
+            eighth = begin + weights[1] * second + weights[2] * third
+            return dot(left_own[own, eighth], right_own[spot]) + dot(
+                left_in[near, which, near_weights[0] * second + near_weights[1] * third],
+                right_in[spot],
             )
+
+        def fill(value):
+            for third in range(2):
+                part = slice(third * cfg.eighth, (third + 1) * cfg.eighth)
+                stage_send[0][slot, part, :] = value(1 - second_bit, third).astype(BF)
+            stage_copy(0, chunk, slot, stage_target(0, chunk)).start()
+            for third in range(2):
+                part = slice(third * cfg.eighth, (third + 1) * cfg.eighth)
+                stage_own[0][slot, part, :] = value(second_bit, third)
+
+        own = 2 * tail_part + which
+        near = lookup(
+            [cfg.near.index(axes[0]) for axes in AXES[: cfg.ff_chunks]] + [len(cfg.near)], block
+        )
 
         @pl.when(chunk < cfg.chunks - 1)
         def _():
-            stage_send[0][slot] = product(which, 1 - second_bit).astype(BF)
-            stage_copy(0, chunk, stage_target(0, chunk)).start()
-            stage_own[0][slot] = product(which, second_bit)
+            fill(functools.partial(product, own, near))
 
         @pl.when(chunk == cfg.chunks - 1)
         def _():
-            left_share(3).wait()
-            split = lax.broadcasted_iota(jnp.int32, (cfg.quarter, CW), 1) < CW - hw
-
-            def mixed(quarter):
-                return jnp.where(split, product(2, quarter), product(3, quarter))
-
-            stage_send[0][slot] = mixed(1 - second_bit).astype(BF)
-            stage_copy(0, chunk, stage_target(0, chunk)).start()
-            stage_own[0][slot] = mixed(second_bit)
-
-    def halve(k, chunk):
-        slot = lax.rem(chunk, SLOTS)
-        stage_copy(k - 1, chunk, stage_target(k - 1, chunk)).wait()
+            split = lax.broadcasted_iota(jnp.int32, (cfg.eighth, CW), 1) < CW - hw
+
+            def mixed(second, third):
+                eighth = begin + weights[1] * second + weights[2] * third
+                parts = [
+                    dot(left_own[2 + index, eighth], right_own[spot])
+                    + dot(
+                        left_in[
+                            len(cfg.near),
+                            index,
+                            near_weights[0] * second + near_weights[1] * third,
+                        ],
+                        right_in[spot],
+                    )
+                    for index in range(2)
+                ]
+                return jnp.where(split, *parts)
+
+            fill(mixed)
+
+    def halve(k, chunk, slot):
+        stage_copy(k - 1, chunk, slot, stage_target(k - 1, chunk)).wait()
         if k == stages:
             result = stage_own[k - 1][slot] + stage_in[k - 1][chunk].astype(F32)
 
@@ -668,10 +783,10 @@
             return stage_own[k - 1][slot, part, :] + stage_in[k - 1][chunk, part, :].astype(F32)
 
         stage_send[k][slot] = total(1 - mine).astype(BF)
-        stage_copy(k, chunk, stage_target(k, chunk)).start()
+        stage_copy(k, chunk, slot, stage_target(k, chunk)).start()
         stage_own[k][slot] = total(mine)
 
-    last_ff = FF_TICKS * (cfg.ff_chunks - 1)
+    last_ff = FF_TICKS[-1]
     pieces = [exchange_sums, norm_two_back, attention_back, norm_one_sums, finish_rows]
     pieces = [(last_ff + index, piece) for index, piece in enumerate(pieces)]
     for k in range(cfg.bits + 1):
@@ -679,32 +794,31 @@
     ticks = max(LAG + cfg.chunks + GAP * stages, pieces[-1][0] + 1)
 
     def tick(t, carry):
+        ff_now = sum(jnp.where(t == when, 1, 0) for when in FF_TICKS)
+        ff_done = sum(jnp.where(t > when, 1, 0) for when in FF_TICKS)
+
+        @pl.when(ff_now > 0)
+        def _():
+            feed_forward(ff_done)
+
         for k in range(stages, 0, -1):
-            chunk = t - LAG - GAP * k
-
-            @pl.when(jnp.logical_and(chunk >= 0, chunk < cfg.chunks))
-            def _(k=k, chunk=chunk):
-                halve(k, chunk)
+            spot = t - LAG - GAP * k
+
+            @pl.when(jnp.logical_and(spot >= 0, spot < cfg.chunks))
+            def _(k=k, spot=spot):
+                halve(k, lookup(cfg.order, spot), lax.rem(spot, SLOTS))
 
         new = t - LAG
 
         @pl.when(jnp.logical_and(new >= 0, new < cfg.chunks))
         def _():
-            form(new)
-
-        @pl.when(jnp.logical_and(lax.rem(t, FF_TICKS) == 0, t <= last_ff))
-        def _():
-            feed_forward(lax.div(t, FF_TICKS))
+            form(lookup(cfg.order, new), lax.rem(new, SLOTS))
 
         for when, piece in pieces:
 
             @pl.when(t == when)
             def _(piece=piece):
                 piece()
-
-        @pl.when(t < cfg.chunks)
-        def _():
-            right_copy(t).start()
 
         return carry
 
@@ -826,13 +940,13 @@
         pltpu.VMEM((cfg.heads, seq, seq), F32),
         pltpu.VMEM((2, hw, seq), BF),
         pltpu.VMEM((cfg.tall, seq), F32),
-        pltpu.VMEM((4, 2, 2, cfg.quarter, seq), BF),
-        pltpu.VMEM((4, 2, cfg.quarter, seq), BF),
-        pltpu.VMEM((cfg.chunks, seq, CW), BF),
-        pltpu.VMEM((cfg.chunks, seq, CW), BF),
+        pltpu.VMEM((4, 8, cfg.eighth, seq), BF),
+        pltpu.VMEM((len(cfg.near) + 1, 2, 4, cfg.eighth, seq), BF),
+        pltpu.VMEM((len(cfg.near), 2, seq, width), BF),
+        pltpu.VMEM((RING + cfg.chunks - cfg.ff_total, seq, CW), BF),
+        pltpu.VMEM((RING + cfg.chunks - cfg.ff_total, seq, CW), BF),
         pltpu.VMEM((width, seq), F32),
         pltpu.VMEM((cfg.tall, seq), F32),
-        pltpu.VMEM((width, seq), BF),
         pltpu.VMEM((width, seq), BF),
         pltpu.VMEM((width, rows), BF),
         pltpu.VMEM((width, rows), BF),
@@ -852,14 +966,18 @@
     scratch += [
         dma((6,)),
         dma((2, 3)),
-        dma((7,)),
-        dma((7,)),
-        dma((4,)),
-        dma((4,)),
-        dma((4,)),
-        dma((4,)),
-        dma((cfg.chunks,)),
-        dma((cfg.chunks,)),
+        dma((8,)),
+        dma((8,)),
+        dma((2,)),
+        dma((2,)),
+        dma((2,)),
+        dma((2,)),
+        dma((3, 2)),
+        dma((3, 2)),
+        dma((3, 2)),
+        dma((3, 2)),
+        dma((cfg.chunks - cfg.ff_total,)),
+        dma((cfg.chunks - cfg.ff_total,)),
         dma((stages, SLOTS)),
         dma((stages, cfg.chunks)),
         dma((cfg.bits + 1,)),
@@ -906,7 +1024,7 @@
         out_specs=[vmem] * 8,
         scratch_shapes=scratch,
         compiler_params=pltpu.CompilerParams(
-            collective_id=0, has_side_effects=True, vmem_limit_bytes=60 * 1024 * 1024
+            collective_id=0, has_side_effects=True, vmem_limit_bytes=62 * 1024 * 1024
         ),
         cost_estimate=pl.CostEstimate(
             flops=14 * 10**9, bytes_accessed=24 * 10**6, transcendentals=10**6
@@ -956,7 +1074,7 @@
             + (layer_out, input_grad, query_sum, key_sum, value_sum, output_sum)
         ]
         + [dma((9,)), dma((9,))],
-        compiler_params=pltpu.CompilerParams(vmem_limit_bytes=16 * 1024 * 1024),
+        compiler_params=pltpu.CompilerParams(vmem_limit_bytes=62 * 1024 * 1024),
     )(
         layer_out,
         input_grad,

time: 141 us -> 123 us (0.87)
  Pallas kernels: 131 us -> 122 us
  local copies, waits for them, and re-layouts: 8.12 us -> 0 us
    pallas_call x1, Pallas kernels: 127 us -> 118 us  [shards(): pl.pallas_call(functools.partial(layer_kernel, cfg), out_shape=[jax.Shape...]
    unnamed x18 -> x0, local copies, waits for them, and re-layouts: 8.12 us -> none
where the time goes in v5:
time: 123 us
  Pallas kernels  122 us (99%)
    pallas_call x1, Pallas kernels, shards(): pl.pallas_call(functools.partial(layer_kernel, cfg), out_shape=[jax.Shape...  118 us
    pallas_call x1, Pallas kernels, shards(): pl.pallas_call(functools.partial(finish_kernel, cfg), out_shape=[like(lay...  4.52 us

profile of v5, /device:TPU:0, one launch (start us, length us, event | category | flops | bytes accessed | tf_op | source)
XLA Modules:
  0.0 122.8 jit_solution(2578198889957268218)
XLA Ops:
  0.6 117.6 %shard_map.238 = (f32[1472,128]{1,0:T(8,128)}, f32[1472,128]{1,0:T(8,128)}, f32[8,768]{1,0:T(8,128)}, f32[3,92,1792]{2,1,0:T(8,128)}, f32[92,192]{1,0:T(8,128)},...) custom-call(bf16[1472,128]{1,0:T(8,128)(2,1)} %bitcast.18, f32[1472]{0:T(1024)} %gain_one.1, ...), custom_call_target="tpu_custom_call" | custom-call | flops 14000000000 | bytes 24000000 | tf_op jit(solution)/shard_map/pallas_call | solution.py:995
  118.3 4.5 %shard_map.239 = (f32[1472,128]{1,0:T(8,128)}, f32[1472,128]{1,0:T(8,128)}, f32[1472]{0:T(1024)}, f32[92,192]{1,0:T(8,128)}, f32[92,192]{1,0:T(8,128)}, /*index=...) custom-call(f32[1472,128]{1,0:T(8,128)} %get-tuple-element.32.layer_, ...), custom_call_target="tpu_custom_call" | custom-call | tf_op jit(solution)/shard_map/pallas_call | solution.py:1053

commit v6 on v5

--- a/solution.py
+++ b/solution.py
@@ -13,11 +13,11 @@
 EPS = 1e-06
 AXES = ((1, 0, 2), (1, 2, 0), (2, 1, 0), (2, 1, 0), (2, 0, 1), (2, 1, 0), (1, 0, 2), (2, 1, 0))
 TOGETHER = (2, 3, 2)
-FF_TICKS = (0, 1, 4, 7, 8, 10, 12)
+OWN_TICKS = (0, 1, 5, 8, 10, 11, 13)
+NEAR_TICKS = (2, 3, 6, 9, 10, 12, 14)
 RING_BLOCKS = 5
-LAG = 0
-GAP = 4
-SLOTS = GAP + 1
+LAG = 2
+GAPS = (4, 4, 4)
 RING = 3 * RING_BLOCKS
 SMALL_GAP = 3
 STEP = 64
@@ -86,6 +86,8 @@
         self.half = -(-width // 256) * 128
         self.tall = width + self.shard_pad
         self.eighth = self.quarter // 2
+        self.gaps = [GAPS[min(k, 2)] for k in range(self.stages)]
+        self.late = [sum(self.gaps[:k]) for k in range(self.stages + 1)]
         self.order = []
         begin = 0
         for count in TOGETHER:
@@ -481,28 +483,29 @@
     build_left(trans, 1)
     small[...] = jnp.zeros_like(small)
 
-    def feed_forward(chunk):
+    def activations(chunk, normed, grad_rows, target):
         slot = lax.rem(chunk, 2)
+        first = lax.rem(3 * chunk, RING)
+        gate = dot(normed, wg[slot])
+        up = dot(normed, wu[slot])
+        grad_hidden = dot(grad_rows, wd[slot])
+        square = gate * gate
+        tanh = jnp.tanh(GELU_C * (gate + 0.044715 * (square * gate)))
+        half = 0.5 * (1.0 + tanh)
+        gelu = gate * half
+        slope = half + (0.5 * GELU_C) * gate * (1.0 - tanh * tanh) * (
+            1.0 + (3 * 0.044715) * square
+        )
+        target[first] = (gelu * up).astype(BF)
+        target[first + 1] = (grad_hidden * up * slope).astype(BF)
+        target[first + 2] = (grad_hidden * gelu).astype(BF)
+
+    def forward_own(chunk):
+        slot = lax.rem(chunk, 2)
+        first = lax.rem(3 * chunk, RING)
         for load in weight_loads(chunk, slot):
             load.wait()
-        first = lax.rem(3 * chunk, RING)
-
-        def activations(normed, grad_rows, target):
-            gate = dot(normed, wg[slot])
-            up = dot(normed, wu[slot])
-            grad_hidden = dot(grad_rows, wd[slot])
-            square = gate * gate
-            tanh = jnp.tanh(GELU_C * (gate + 0.044715 * (square * gate)))
-            half = 0.5 * (1.0 + tanh)
-            gelu = gate * half
-            slope = half + (0.5 * GELU_C) * gate * (1.0 - tanh * tanh) * (
-                1.0 + (3 * 0.044715) * square
-            )
-            target[first] = (gelu * up).astype(BF)
-            target[first + 1] = (grad_hidden * up * slope).astype(BF)
-            target[first + 2] = (grad_hidden * gelu).astype(BF)
-
-        activations(normed_two[...], cot[...], right_own)
+        activations(chunk, normed_two[...], cot[...], right_own)
         hidden, grad_gate, grad_up = (right_own[first + kind] for kind in range(3))
         for block in blocks_of(width, MROWS):
             out_acc[block, :] += dot_nt(wd[slot, block, :], hidden)
@@ -510,15 +513,16 @@
                 wu[slot, block, :], grad_up
             )
 
+    def forward_near(chunk):
+        slot = lax.rem(chunk, 2)
         for near, use in enumerate(cfg.first_use):
 
             @pl.when(chunk == use)
             def _(near=near):
-                adopt(near, 0)
                 adopt(near, 1)
 
         near = lookup([cfg.near.index(axes[0]) for axes in AXES[: cfg.ff_chunks]], chunk)
-        activations(near_rows[near, 1], near_rows[near, 0], right_in)
+        activations(chunk, near_rows[near, 1], near_rows[near, 0], right_in)
 
         @pl.when(chunk < cfg.ff_chunks - 2)
         def _():
@@ -537,13 +541,9 @@
         return (lax.div(lane, rows) == core).astype(F32)
 
     def lane_sums(weights, source):
-        return lax.dot_general(
-            weights,
-            source,
-            (((1,), (1,)), ((), ())),
-            precision=lax.Precision.HIGHEST,
-            preferred_element_type=F32,
-        )[0:1, :]
+        high = source.astype(BF)
+        low = (source - high.astype(F32)).astype(BF)
+        return (dot_nt(weights.astype(BF), high) + dot_nt(weights.astype(BF), low))[0:1, :]
 
     def put_small(row, line):
         small[row : row + 1, :] = line[:, : cfg.half]
@@ -674,7 +674,11 @@
             small[...] = small[...] + small_in[k]
             small_copy(k + 1).start()
 
-    def stage_copy(k, chunk, slot, target):
+    def slot_of(k, spot):
+        return lax.rem(spot, cfg.gaps[k] + 1)
+
+    def stage_copy(k, chunk, spot, target):
+        slot = slot_of(k, spot)
         return send(
             stage_send[k].at[slot],
             stage_in[k].at[chunk],
@@ -686,7 +690,8 @@
     def stage_target(k, chunk):
         return pick(chunk, k + 1, peer)
 
-    def form(chunk, slot):
+    def form(chunk, position):
+        slot = slot_of(0, position)
         tail_part = lax.div(chunk, cfg.ff_total)
         which = (1 - tail_part) * lax.div(lax.rem(chunk, 3) + 1, 2)
         block = block_of(chunk)
@@ -713,21 +718,30 @@
             def _(index=index):
                 right_copy(index).wait()
 
-        def product(own, near, second, third):
-            eighth = begin + weights[1] * second + weights[2] * third
-            return dot(left_own[own, eighth], right_own[spot]) + dot(
-                left_in[near, which, near_weights[0] * second + near_weights[1] * third],
-                right_in[spot],
+        parts = [(second, third) for second in (1 - second_bit, second_bit) for third in range(2)]
+
+        def product(own, near, index):
+            left = [
+                jnp.concatenate(
+                    [left_own[own, begin + weights[1] * s + weights[2] * t] for s, t in parts], axis=0
+                ),
+                jnp.concatenate(
+                    [
+                        left_in[near, index, near_weights[0] * s + near_weights[1] * t]
+                        for s, t in parts
+                    ],
+                    axis=0,
+                ),
+            ]
+            return dot(
+                jnp.concatenate(left, axis=1),
+                jnp.concatenate([right_own[spot], right_in[spot]], axis=0),
             )
 
-        def fill(value):
-            for third in range(2):
-                part = slice(third * cfg.eighth, (third + 1) * cfg.eighth)
-                stage_send[0][slot, part, :] = value(1 - second_bit, third).astype(BF)
-            stage_copy(0, chunk, slot, stage_target(0, chunk)).start()
-            for third in range(2):
-                part = slice(third * cfg.eighth, (third + 1) * cfg.eighth)
-                stage_own[0][slot, part, :] = value(second_bit, third)
+        def fill(sums):
+            stage_send[0][slot] = sums[: cfg.quarter, :].astype(BF)
+            stage_copy(0, chunk, position, stage_target(0, chunk)).start()
+            stage_own[0][slot] = sums[cfg.quarter :, :]
 
         own = 2 * tail_part + which
         near = lookup(
@@ -736,34 +750,18 @@
 
         @pl.when(chunk < cfg.chunks - 1)
         def _():
-            fill(functools.partial(product, own, near))
+            fill(product(own, near, which))
 
         @pl.when(chunk == cfg.chunks - 1)
         def _():
-            split = lax.broadcasted_iota(jnp.int32, (cfg.eighth, CW), 1) < CW - hw
-
-            def mixed(second, third):
-                eighth = begin + weights[1] * second + weights[2] * third
-                parts = [
-                    dot(left_own[2 + index, eighth], right_own[spot])
-                    + dot(
-                        left_in[
-                            len(cfg.near),
-                            index,
-                            near_weights[0] * second + near_weights[1] * third,
-                        ],
-                        right_in[spot],
-                    )
-                    for index in range(2)
-                ]
-                return jnp.where(split, *parts)
-
-            fill(mixed)
-
-    def halve(k, chunk, slot):
-        stage_copy(k - 1, chunk, slot, stage_target(k - 1, chunk)).wait()
+            split = lax.broadcasted_iota(jnp.int32, (2 * cfg.quarter, CW), 1) < CW - hw
+            fill(jnp.where(split, *(product(2 + index, len(cfg.near), index) for index in range(2))))
+
+    def halve(k, chunk, position):
+        stage_copy(k - 1, chunk, position, stage_target(k - 1, chunk)).wait()
+        old = slot_of(k - 1, position)
         if k == stages:
-            result = stage_own[k - 1][slot] + stage_in[k - 1][chunk].astype(F32)
+            result = stage_own[k - 1][old] + stage_in[k - 1][chunk].astype(F32)
 
             @pl.when(chunk < cfg.ff_total)
             def _():
@@ -780,39 +778,46 @@
 
         def total(which):
             part = pl.ds(pl.multiple_of(which * half, 16), half)
-            return stage_own[k - 1][slot, part, :] + stage_in[k - 1][chunk, part, :].astype(F32)
-
+            return stage_own[k - 1][old, part, :] + stage_in[k - 1][chunk, part, :].astype(F32)
+
+        slot = slot_of(k, position)
         stage_send[k][slot] = total(1 - mine).astype(BF)
-        stage_copy(k, chunk, slot, stage_target(k, chunk)).start()
+        stage_copy(k, chunk, position, stage_target(k, chunk)).start()
         stage_own[k][slot] = total(mine)
 
-    last_ff = FF_TICKS[-1]
+    last_ff = OWN_TICKS[-1]
     pieces = [exchange_sums, norm_two_back, attention_back, norm_one_sums, finish_rows]
     pieces = [(last_ff + index, piece) for index, piece in enumerate(pieces)]
     for k in range(cfg.bits + 1):
         pieces.append((pieces[-1][0] + SMALL_GAP, functools.partial(small_stage, k)))
-    ticks = max(LAG + cfg.chunks + GAP * stages, pieces[-1][0] + 1)
+    ticks = max(LAG + cfg.chunks + cfg.late[stages], pieces[-1][0] + 1)
 
     def tick(t, carry):
-        ff_now = sum(jnp.where(t == when, 1, 0) for when in FF_TICKS)
-        ff_done = sum(jnp.where(t > when, 1, 0) for when in FF_TICKS)
-
-        @pl.when(ff_now > 0)
+        for ticks_of, forward in ((OWN_TICKS, forward_own), (NEAR_TICKS, forward_near)):
+            now = sum(jnp.where(t == when, 1, 0) for when in ticks_of)
+            past = sum(jnp.where(t > when, 1, 0) for when in ticks_of)
+
+            @pl.when(now > 0)
+            def _(forward=forward, past=past):
+                forward(past)
+
+        @pl.when(t == NEAR_TICKS[0] - 1)
         def _():
-            feed_forward(ff_done)
+            for near in range(len(cfg.near)):
+                adopt(near, 0)
 
         for k in range(stages, 0, -1):
-            spot = t - LAG - GAP * k
+            spot = t - LAG - cfg.late[k]
 
             @pl.when(jnp.logical_and(spot >= 0, spot < cfg.chunks))
             def _(k=k, spot=spot):
-                halve(k, lookup(cfg.order, spot), lax.rem(spot, SLOTS))
+                halve(k, lookup(cfg.order, spot), spot)
 
         new = t - LAG
 
         @pl.when(jnp.logical_and(new >= 0, new < cfg.chunks))
         def _():
-            form(lookup(cfg.order, new), lax.rem(new, SLOTS))
+            form(lookup(cfg.order, new), new)
 
         for when, piece in pieces:
 
@@ -959,8 +964,10 @@
         pltpu.VMEM((cfg.chunks - cfg.ff_total, cfg.shard_pad, CW), F32),
         pltpu.VMEM((1, 2 * seq), jnp.int32),
     ]
-    scratch += [pltpu.VMEM((SLOTS, size, CW), F32) for size in cfg.stage_rows]
-    scratch += [pltpu.VMEM((SLOTS, size, CW), BF) for size in cfg.stage_rows]
+    for dtype in (F32, BF):
+        scratch += [
+            pltpu.VMEM((gap + 1, size, CW), dtype) for gap, size in zip(cfg.gaps, cfg.stage_rows)
+        ]
     scratch += [pltpu.VMEM((cfg.chunks, size, CW), BF) for size in cfg.stage_rows]
     dma = pltpu.SemaphoreType.DMA
     scratch += [
@@ -978,7 +985,7 @@
         dma((3, 2)),
         dma((cfg.chunks - cfg.ff_total,)),
         dma((cfg.chunks - cfg.ff_total,)),
-        dma((stages, SLOTS)),
+        dma((stages, max(cfg.gaps) + 1)),
         dma((stages, cfg.chunks)),
         dma((cfg.bits + 1,)),
         dma((cfg.bits + 1,)),

time: 123 us -> 117 us (0.951)
  Pallas kernels: 122 us -> 116 us
    pallas_call x1, Pallas kernels: 118 us -> 111 us  [shards(): pl.pallas_call(functools.partial(layer_kernel, cfg), out_shape=[jax.Shape...]
where the time goes in v6:
time: 117 us; the launch traced here: 116 us
  Pallas kernels  116 us (99%)
    pallas_call x1, Pallas kernels, shards(): pl.pallas_call(functools.partial(layer_kernel, cfg), out_shape=[jax.Shape...  111 us
    pallas_call x1, Pallas kernels, shards(): pl.pallas_call(functools.partial(finish_kernel, cfg), out_shape=[like(lay...  4.52 us

profile of v6, /device:TPU:0, one launch (start us, length us, event | category | flops | bytes accessed | tf_op | source)
XLA Modules:
  0.0 116.3 jit_solution(4208953066892470193)
XLA Ops:
  0.6 111.1 %shard_map.238 = (f32[1472,128]{1,0:T(8,128)}, f32[1472,128]{1,0:T(8,128)}, f32[8,768]{1,0:T(8,128)}, f32[3,92,1792]{2,1,0:T(8,128)}, f32[92,192]{1,0:T(8,128)},...) custom-call(bf16[1472,128]{1,0:T(8,128)(2,1)} %bitcast.18, f32[1472]{0:T(1024)} %gain_one.1, ...), custom_call_target="tpu_custom_call" | custom-call | flops 14000000000 | bytes 24000000 | tf_op jit(solution)/shard_map/pallas_call | solution.py:1002
  111.8 4.5 %shard_map.239 = (f32[1472,128]{1,0:T(8,128)}, f32[1472,128]{1,0:T(8,128)}, f32[1472]{0:T(1024)}, f32[92,192]{1,0:T(8,128)}, f32[92,192]{1,0:T(8,128)}, /*index=...) custom-call(f32[1472,128]{1,0:T(8,128)} %get-tuple-element.32.layer_, ...), custom_call_target="tpu_custom_call" | custom-call | tf_op jit(solution)/shard_map/pallas_call | solution.py:1060

commit v7 on v6

--- a/solution.py
+++ b/solution.py
@@ -115,10 +115,10 @@
     lengths,
     groups,
     bucket_ids,
-    layer_out,
-    input_grad,
+    layer_hbm,
+    input_hbm,
     small_out,
-    ff_out,
+    ff_hbm,
     query_out,
     key_out,
     value_out,
@@ -158,6 +158,9 @@
     small_in,
     att_final,
     ids_row,
+    layer_out,
+    input_grad,
+    ff_out,
     *rest,
 ):
     grad_send = normed_one
@@ -184,6 +187,7 @@
         stage_recv_sem,
         small_send_sem,
         small_recv_sem,
+        out_sem,
     ) = rest[3 * stages :]
 
     seq, rows, width, hw, heads = cfg.seq, cfg.local_rows, cfg.width, cfg.head_width, cfg.heads
@@ -442,18 +446,25 @@
         attended[core, part, :] = dot(qkv[2, part, :], prob.astype(BF)).astype(BF)
     pair_att.start()
 
-    build_left(trans, 2)
-    pair_cot.wait()
-    pair_rows.wait()
     row_valid = lax.broadcasted_iota(jnp.int32, (step_rows, seq), 1) < group_len
 
-    def mask_rows(step, carry):
-        block = rows_at(step)
-        trans[block, :] = jnp.where(row_valid, whole(cot_raw, block).astype(F32), 0.0)
-        return carry
-
-    lax.fori_loop(0, steps, mask_rows, 0)
-    build_left(trans, 0)
+    def build_argument_lefts():
+        def first_rows(step, carry):
+            block = rows_at(step)
+            trans[block, :] = normed_one[block, :].astype(F32)
+            return carry
+
+        lax.fori_loop(0, steps, first_rows, 0)
+        build_left(trans, 2)
+        pair_cot.wait()
+
+        def mask_rows(step, carry):
+            block = rows_at(step)
+            trans[block, :] = jnp.where(row_valid, whole(cot_raw, block).astype(F32), 0.0)
+            return carry
+
+        lax.fori_loop(0, steps, mask_rows, 0)
+        build_left(trans, 0)
 
     loads[5].wait()
     pair_wo.wait()
@@ -481,6 +492,7 @@
     for near in range(len(cfg.near)):
         near_copy(near, 1).start()
     build_left(trans, 1)
+    pair_rows.wait()
     small[...] = jnp.zeros_like(small)
 
     def activations(chunk, normed, grad_rows, target):
@@ -623,6 +635,18 @@
                 dot_tn(wqkv[part, :, block], grad_qkv[part, :, own_lanes]) for part in range(3)
             )
 
+    row_stores = [
+        pltpu.make_async_copy(src, dst, out_sem.at[cfg.ff_total + index])
+        for index, (src, dst) in enumerate(((layer_out, layer_hbm), (input_grad, input_hbm)))
+    ]
+
+    def ff_store(chunk):
+        columns = pl.ds(pl.multiple_of(lax.div(chunk, 3) * CW, CW), CW)
+        kind = lax.rem(chunk, 3)
+        return pltpu.make_async_copy(
+            ff_out.at[kind, :, columns], ff_hbm.at[kind, :, columns], out_sem.at[chunk]
+        )
+
     def small_copy(k):
         target = sibling if k == cfg.bits else (peer[k], core)
         return send(
@@ -664,6 +688,8 @@
         lax.fori_loop(0, steps, last_rows, 0)
         put_small(0, lane_sums(jnp.ones((8, rows), F32), trans[:width, :rows]))
         small_copy(0).start()
+        for store in row_stores:
+            store.start()
 
     def small_stage(k):
         small_copy(k).wait()
@@ -767,6 +793,7 @@
             def _():
                 columns = pl.ds(pl.multiple_of(lax.div(chunk, 3) * CW, CW), CW)
                 ff_out[lax.rem(chunk, 3), :, columns] = result[: cfg.shard, :]
+                ff_store(chunk).start()
 
             @pl.when(chunk >= cfg.ff_total)
             def _():
@@ -803,6 +830,7 @@
 
         @pl.when(t == NEAR_TICKS[0] - 1)
         def _():
+            build_argument_lefts()
             for near in range(len(cfg.near)):
                 adopt(near, 0)
 
@@ -833,6 +861,14 @@
     for part, ref in enumerate((query_out, key_out, value_out)):
         ref[...] = flat[: cfg.shard, part * hw : (part + 1) * hw]
     output_out[...] = jnp.transpose(flat[:, 3 * hw :])[:, : cfg.shard]
+    for store in row_stores:
+        store.wait()
+
+    def wait_store(chunk, carry):
+        ff_store(chunk).wait()
+        return carry
+
+    lax.fori_loop(0, cfg.ff_total, wait_store, 0)
 
 
 def finish_kernel(
@@ -878,9 +914,6 @@
         stores.append(pltpu.make_async_copy(buffer, dst, store_sem.at[index]))
     for load in loads:
         load.start()
-    for load, store in zip(loads, stores):
-        load.wait()
-        store.start()
     for row, gain in ((0, gain_one), (2, gain_two)):
         line = jnp.concatenate([small[row : row + 1, :], small[row + 1 : row + 2, :]], axis=1)
         gain[...] = line[:, : cfg.width].reshape(cfg.width)
@@ -895,6 +928,9 @@
         preferred_element_type=F32,
     )
     bias_out[...] = sums[4 : 4 + cfg.heads, :]
+    for load, store in zip(loads, stores):
+        load.wait()
+        store.start()
     for store in stores:
         store.wait()
 
@@ -963,6 +999,9 @@
         pltpu.VMEM((cfg.bits + 1,) + small_shape, F32),
         pltpu.VMEM((cfg.chunks - cfg.ff_total, cfg.shard_pad, CW), F32),
         pltpu.VMEM((1, 2 * seq), jnp.int32),
+        pltpu.VMEM((width, rows), F32),
+        pltpu.VMEM((width, rows), F32),
+        pltpu.VMEM((3, shard, hidden), F32),
     ]
     for dtype in (F32, BF):
         scratch += [
@@ -989,6 +1028,7 @@
         dma((stages, cfg.chunks)),
         dma((cfg.bits + 1,)),
         dma((cfg.bits + 1,)),
+        dma((cfg.ff_total + 2,)),
     ]
     (
         layer_out,
@@ -1028,7 +1068,7 @@
             smem,
             vmem,
         ],
-        out_specs=[vmem] * 8,
+        out_specs=[any_spec, any_spec, vmem, any_spec] + [vmem] * 4,
         scratch_shapes=scratch,
         compiler_params=pltpu.CompilerParams(
             collective_id=0, has_side_effects=True, vmem_limit_bytes=62 * 1024 * 1024

time: 117 us -> 116 us (level)
  no operation moved by 1% of the time
where the time goes in v7:
time: 116 us
  Pallas kernels  115 us (99%)
    pallas_call x1, Pallas kernels, shards(): pl.pallas_call(functools.partial(layer_kernel, cfg), out_shape=[jax.Shape...  110 us
    pallas_call x1, Pallas kernels, shards(): pl.pallas_call(functools.partial(finish_kernel, cfg), out_shape=[like(lay...  4.52 us

profile of v7, /device:TPU:0, one launch (start us, length us, event | category | flops | bytes accessed | tf_op | source)
XLA Modules:
  0.0 115.6 jit_solution(17400367645466233605)
XLA Ops:
  0.6 110.5 %shard_map.238 = (f32[1472,128]{1,0:T(8,128)}, f32[1472,128]{1,0:T(8,128)}, f32[8,768]{1,0:T(8,128)}, f32[3,92,1792]{2,1,0:T(8,128)}, f32[92,192]{1,0:T(8,128)},...) custom-call(bf16[1472,128]{1,0:T(8,128)(2,1)} %bitcast.18, f32[1472]{0:T(1024)} %gain_one.1, ...), custom_call_target="tpu_custom_call" | custom-call | flops 14000000000 | bytes 24000000 | tf_op jit(solution)/shard_map/pallas_call | solution.py:1042
  111.1 4.5 %shard_map.239 = (f32[1472,128]{1,0:T(8,128)}, f32[1472,128]{1,0:T(8,128)}, f32[1472]{0:T(1024)}, f32[92,192]{1,0:T(8,128)}, f32[92,192]{1,0:T(8,128)}, /*index=...) custom-call(f32[1472,128]{1,0:T(8,128)} %get-tuple-element.32.layer_, ...), custom_call_target="tpu_custom_call" | custom-call | tf_op jit(solution)/shard_map/pallas_call | solution.py:1100

commit v8 on v7

--- a/solution.py
+++ b/solution.py
@@ -13,7 +13,7 @@
 EPS = 1e-06
 AXES = ((1, 0, 2), (1, 2, 0), (2, 1, 0), (2, 1, 0), (2, 0, 1), (2, 1, 0), (1, 0, 2), (2, 1, 0))
 TOGETHER = (2, 3, 2)
-OWN_TICKS = (0, 1, 5, 8, 10, 11, 13)
+OWN_TICKS = (0, 1, 4, 7, 9, 11, 13)
 NEAR_TICKS = (2, 3, 6, 9, 10, 12, 14)
 RING_BLOCKS = 5
 LAG = 2
@@ -318,7 +318,7 @@
         axis = cfg.near[near]
         high, low = (k for k in (2, 1, 0) if k != axis)
         for block in blocks_of(width, 128):
-            trans[block, :] = jnp.transpose(near_rows[near, which, :, block].astype(F32))
+            trans[block, :] = jnp.transpose(near_rows[near, which, :, block]).astype(F32)
         for value in range(2):
 
             @pl.when(bit[axis] == value)
@@ -701,7 +701,7 @@
             small_copy(k + 1).start()
 
     def slot_of(k, spot):
-        return lax.rem(spot, cfg.gaps[k] + 1)
+        return spot % (cfg.gaps[k] + 1) if isinstance(spot, int) else lax.rem(spot, cfg.gaps[k] + 1)
 
     def stage_copy(k, chunk, spot, target):
         slot = slot_of(k, spot)
@@ -712,6 +712,11 @@
             stage_recv_sem.at[k, chunk],
             (target, core),
         )
+
+    def free_slot(k, chunk, position):
+        @pl.when(position > cfg.gaps[k])
+        def _():
+            stage_copy(k, chunk, position, peer[0]).wait_send()
 
     def stage_target(k, chunk):
         return pick(chunk, k + 1, peer)
@@ -765,6 +770,7 @@
             )
 
         def fill(sums):
+            free_slot(0, chunk, position)
             stage_send[0][slot] = sums[: cfg.quarter, :].astype(BF)
             stage_copy(0, chunk, position, stage_target(0, chunk)).start()
             stage_own[0][slot] = sums[cfg.quarter :, :]
@@ -784,7 +790,7 @@
             fill(jnp.where(split, *(product(2 + index, len(cfg.near), index) for index in range(2))))
 
     def halve(k, chunk, position):
-        stage_copy(k - 1, chunk, position, stage_target(k - 1, chunk)).wait()
+        stage_copy(k - 1, chunk, position, stage_target(k - 1, chunk)).wait_recv()
         old = slot_of(k - 1, position)
         if k == stages:
             result = stage_own[k - 1][old] + stage_in[k - 1][chunk].astype(F32)
@@ -808,6 +814,7 @@
             return stage_own[k - 1][old, part, :] + stage_in[k - 1][chunk, part, :].astype(F32)
 
         slot = slot_of(k, position)
+        free_slot(k, chunk, position)
         stage_send[k][slot] = total(1 - mine).astype(BF)
         stage_copy(k, chunk, position, stage_target(k, chunk)).start()
         stage_own[k][slot] = total(mine)
@@ -856,6 +863,10 @@
         return carry
 
     lax.fori_loop(0, ticks, tick, 0)
+
+    for k in range(stages):
+        for position in range(cfg.chunks - cfg.gaps[k] - 1, cfg.chunks):
+            stage_copy(k, cfg.order[position], position, peer[0]).wait_send()
 
     flat = jnp.concatenate([att_final[index] for index in range(cfg.chunks - cfg.ff_total)], axis=1)
     for part, ref in enumerate((query_out, key_out, value_out)):

time: 116 us -> 117 us (level)
  no operation moved by 1% of the time
where the time goes in v8:
time: 117 us; the launch traced here: 116 us
  Pallas kernels  116 us (99%)
    pallas_call x1, Pallas kernels, shards(): pl.pallas_call(functools.partial(layer_kernel, cfg), out_shape=[jax.Shape...  111 us
    pallas_call x1, Pallas kernels, shards(): pl.pallas_call(functools.partial(finish_kernel, cfg), out_shape=[like(lay...  4.52 us

profile of v8, /device:TPU:0, one launch (start us, length us, event | category | flops | bytes accessed | tf_op | source)
XLA Modules:
  0.0 116.4 jit_solution(17539856244882717393)
XLA Ops:
  0.6 111.2 %shard_map.238 = (f32[1472,128]{1,0:T(8,128)}, f32[1472,128]{1,0:T(8,128)}, f32[8,768]{1,0:T(8,128)}, f32[3,92,1792]{2,1,0:T(8,128)}, f32[92,192]{1,0:T(8,128)},...) custom-call(bf16[1472,128]{1,0:T(8,128)(2,1)} %bitcast.18, f32[1472]{0:T(1024)} %gain_one.1, ...), custom_call_target="tpu_custom_call" | custom-call | flops 14000000000 | bytes 24000000 | tf_op jit(solution)/shard_map/pallas_call | solution.py:1053
  111.9 4.5 %shard_map.239 = (f32[1472,128]{1,0:T(8,128)}, f32[1472,128]{1,0:T(8,128)}, f32[1472]{0:T(1024)}, f32[92,192]{1,0:T(8,128)}, f32[92,192]{1,0:T(8,128)}, /*index=...) custom-call(f32[1472,128]{1,0:T(8,128)} %get-tuple-element.32.layer_, ...), custom_call_target="tpu_custom_call" | custom-call | tf_op jit(solution)/shard_map/pallas_call | solution.py:1111
